TPU v7x, 256 devices: a whole 4x4x8 slice. The times are simulated.
256 devices in a mesh: af: 4 (over x), gx: 16 (over y_lo, z), gy: 4 (over y_hi, core).
Axes of the slice: x: 4, y: 4 (y_hi: 2, y_lo: 2; y = y_hi * 2 + y_lo), z: 8, core: 2. Of those that a mesh axis runs over, the one named last changes fastest.
Arguments:
- fields_state: float32 [32, 6, 64, 64, 128], P('af', None, 'gx', 'gy'), may hold values from -6 to 6
- velocity: float32 [3, 64, 64, 128], P(None, 'gx', 'gy'), may hold values from -3 to 3
- diffusivity: float32 [64, 64, 128], P('gx', 'gy'), may hold values from 0.02 to 0.15
- wiener_draw: float32 [32, 3], P('af'), may hold values from -4 to 4
Outputs:
- next_state: float32 [32, 6, 64, 64, 128], P('af', None, 'gx', 'gy')
All inputs are finite; a program needn't handle non-finite values.
Results may differ from a plain program's by a relative error of at most 0.00002.
Values sent between devices are 32-bit elements; how exact they have to be, the bound alone decides.
A program may use at most 64 MiB of HBM per device.

v0:
```python
import jax
import jax.numpy as jnp
from jax import lax
from jax.sharding import PartitionSpec as P

FIELDS = 32


time_step = 0.3
mix_rate = 4.0
radiation = 0.5
nucleation = (1.0, 0.8, 0.6, 0.5)
growth_rate = 0.5
oxidation = 0.3


def padded_2(cells, sides, width):
    for axis, dim in sides:
        count = lax.axis_size(axis)
        ends = count - 1
        head = lax.slice_in_dim(cells, 0, width, axis=dim)
        tail = lax.slice_in_dim(cells, cells.shape[dim] - width, cells.shape[dim], axis=dim)
        cells = jnp.concatenate(
            [
                lax.ppermute(tail, axis, [(i, (i + 1) % count) for i in range(ends)]),
                cells,
                lax.ppermute(head, axis, [((i + 1) % count, i) for i in range(ends)]),
            ],
            axis=dim,
        )
    return cells


def neighbours_z(values):
    edge = jnp.zeros_like(values[..., :1])
    return (
        jnp.concatenate([values[..., 1:], edge], -1),
        jnp.concatenate([edge, values[..., :-1]], -1),
    )


def soot_sources(centre):
    mixture = centre[..., 0, :, :, :]
    enthalpy = centre[..., 1, :, :, :]
    soot_weight = jax.nn.sigmoid(3.0 * enthalpy) * mixture * mixture / (1.0 + mixture * mixture)
    moments = [centre[..., 2 + moment_index, :, :, :] for moment_index in range(4)]
    source_terms = [jnp.zeros_like(mixture), -radiation * soot_weight]
    for moment_index in range(4):
        moment_rate = nucleation[moment_index] * soot_weight - oxidation * moments[moment_index]
        if moment_index > 0:
            moment_rate = moment_rate + growth_rate * soot_weight * moments[moment_index - 1]
        source_terms.append(moment_rate)
    return jnp.stack(source_terms, axis=-4)


def direction_weight(wiener, direction):
    return wiener[..., direction][..., None, None, None, None]


def tendency(padded, coefficients, field_mean, wiener):
    centre = padded[..., 1:-1, 1:-1, :]
    east_side = padded[..., 2:, 1:-1, :]
    west_side = padded[..., :-2, 1:-1, :]
    north_side = padded[..., 1:-1, 2:, :]
    south_side = padded[..., 1:-1, :-2, :]
    upper_side, lower_side = neighbours_z(centre)
    east_speed = coefficients[0, 2:, 1:-1]
    west_speed = coefficients[0, :-2, 1:-1]
    north_speed = coefficients[1, 1:-1, 2:]
    south_speed = coefficients[1, 1:-1, :-2]
    upper_speed, lower_speed = neighbours_z(coefficients[2, 1:-1, 1:-1])
    diffusion = coefficients[3, 1:-1, 1:-1]
    transport = -0.5 * (
        east_speed * east_side
        - west_speed * west_side
        + (north_speed * north_side - south_speed * south_side)
        + (upper_speed * upper_side - lower_speed * lower_side)
    )
    laplace_sum = (
        east_side + west_side + north_side + south_side + upper_side + lower_side - 6.0 * centre
    )
    stirring = 0.5 * (
        direction_weight(wiener, 0) * (east_side - west_side)
        + direction_weight(wiener, 1) * (north_side - south_side)
        + direction_weight(wiener, 2) * (upper_side - lower_side)
    )
    return (
        transport
        + diffusion * laplace_sum
        + jnp.sqrt(2.0 * diffusion / time_step) * stirring
        - mix_rate * diffusion * (centre - field_mean)
        + soot_sources(centre)
    )


def local(fields_state, velocity, diffusivity, wiener_draw):
    coefficients = jnp.concatenate([velocity, diffusivity[None]], 0)
    coef_pad = padded_2(coefficients, (("gx", 1), ("gy", 2)), 1)

    def advance(section_now, weight_base, weight_section):
        field_sums = lax.psum(jnp.sum(section_now, axis=0), "af")
        field_mean = field_sums / FIELDS
        padded = padded_2(section_now, (("gx", 2), ("gy", 3)), 1)
        change = tendency(padded, coef_pad, field_mean, wiener_draw)
        return weight_base * fields_state + weight_section * (section_now + time_step * change)

    first_section = advance(fields_state, 0.0, 1.0)
    second_section = advance(first_section, 0.75, 0.25)
    return advance(second_section, 1.0 / 3.0, 2.0 / 3.0)


def solution(mesh):
    return jax.shard_map(
        local,
        mesh=mesh,
        in_specs=(
            P("af", None, "gx", "gy", None),
            P(None, "gx", "gy", None),
            P("gx", "gy", None),
            P("af", None),
        ),
        out_specs=P("af", None, "gx", "gy", None),
        check_vma=False,
    )
```

profile of v0, /device:TPU:8, one launch (start us, length us, event | category | flops | bytes accessed | tf_op | source)
XLA Modules:
  0.0 220.9 jit_solution(7313710709457334750)
XLA Ops:
  6.5 0.8 pad_maximum_fusion.36
  7.3 7.6 %collective-permute-start = (f32[4,1,16,128]{3,2,1,0:T(8,128)S(1)}, f32[4,1,16,128]{3,2,1,0:T(8,128)S(1)}, u32[]{:S(2)}, u32[]{:S(2)}) collective-permute-start(f32[4,1,16,128]{3,2,1,0:T(8,128)S(1)} %get-tuple-element.40), channel_id=1, source_target_pairs={{4,0},{8,4},{12,8},{16,12},{20,16},{24,20},{28,24},{32,28},{36,32}... | collective-permute-start | bytes 98312 | tf_op jit(solution)/shard_map/ppermute | solution.py:27
  15.0 1.9 collective-permute-start.2
  16.9 2.3 %copy.5 = f32[8,6,4,16,128]{4,0,3,2,1:T(8,128)S(1)} copy(f32[8,6,4,16,128]{4,3,2,1,0:T(8,128)} %param.4) | data formatting | bytes 3145728 | tf_op args[0]
  19.2 0.9 fusion.56
  20.2 1.9 collective-permute-start.3
  22.1 6.0 %collective-permute-start.1 = (f32[8,6,1,16,128]{4,0,3,2,1:T(8,128)}, f32[8,6,1,16,128]{4,0,3,2,1:T(8,128)}, u32[]{:S(2)}, u32[]{:S(2)}) collective-permute-start(f32[8,6,1,16,128]{4,0,3,2,1:T(8,128)} %get-tuple-element.29), channel_id=1, source_target_pairs={{4,0},{8,4},{12,8},{16,12},{20,16},{24,20},{28,24},{32,28},{36,32}... | collective-permute-start | bytes 1179656 | tf_op jit(solution)/shard_map/ppermute | solution.py:27
  28.1 0.8 reduce_sum.27
  29.0 2.2 %fusion.57 = (f32[8,6,4,16,127]{4,0,3,2,1:T(8,128)}, f32[8,6,4,16,127]{4,0,3,2,1:T(8,128)}) fusion(f32[8,6,4,16,128]{4,0,3,2,1:T(8,128)S(1)} %copy.5), kind=kLoop, calls=%fused_computation.137 | loop fusion | bytes 6242304 | tf_op jit(solution)/shard_map/slice | solution.py:37
  31.3 0.1 multiply_dynamic-update-slice_fusion.2
  31.7 0.5 copy-done.12
  32.2 0.8 broadcast_dynamic-update-slice_fusion.1
  33.0 1.3 collective-permute-start.4
  34.3 3.0 %collective-permute-start.6 = (f32[4,6,1,128]{3,2,1,0:T(1,128)S(1)}, f32[4,6,1,128]{3,2,1,0:T(1,128)S(1)}, u32[]{:S(2)}, u32[]{:S(2)}) collective-permute-start(f32[4,6,1,128]{3,2,1,0:T(1,128)S(1)} %get-tuple-element.36), channel_id=1, source_target_pairs={{0,1},{1,2},{2,3},{4,5},{5,6},{6,7},{8,9},{9,10},{10,11},{12,13},{... | collective-permute-start | bytes 36872 | tf_op jit(solution)/shard_map/ppermute | solution.py:25
  37.4 0.7 broadcast_dynamic-update-slice_fusion
  38.1 0.1 collective-permute-done.6
  38.2 0.1 fusion.58
  38.3 0.1 concatenate.108
  38.4 1.0 constant_dynamic-update-slice_fusion.2
  39.4 0.9 constant_dynamic-update-slice_fusion.1
  40.3 1.0 constant_dynamic-update-slice_fusion
  41.4 1.4 copy-done.2
  42.8 1.3 collective-permute-start.5
  44.1 4.7 %collective-permute-start.7 = (f32[8,6,6,1,128]{4,0,3,2,1:T(8,128)S(1)}, f32[8,6,6,1,128]{4,0,3,2,1:T(8,128)S(1)}, u32[]{:S(2)}, u32[]{:S(2)}) collective-permute-start(f32[8,6,6,1,128]{4,0,3,2,1:T(8,128)S(1)} %get-tuple-element.20), channel_id=1, source_target_pairs={{0,1},{1,2},{2,3},{4,5},{5,6},{6,7},{8,9},{9,10},{10,11},{12,13},{... | collective-permute-start | bytes 442376 | tf_op jit(solution)/shard_map/ppermute | solution.py:25
  48.9 25.1 %all-reduce.12.cloned.1.call-done = f32[6,4,16,128]{3,2,1,0:T(8,128)} async-done(((f32[6,4,16,128]{3,2,1,0:T(8,128)}), f32[6,4,16,128]{3,2,1,0:T(8,128)}) %all-reduce.12.cloned.1.call-update) | async-done | bytes 196624 | tf_op jit(solution)/shard_map/psum | solution.py:101
  73.9 0.9 broadcast_multiply_fusion.2
  74.9 0.6 copy-done.8
  75.6 6.1 %fusion.48 = (f32[6,4,16,128]{3,2,1,0:T(8,128)}, f32[8,6,4,16,128]{4,0,3,2,1:T(8,128)S(1)}) fusion(f32[8,6,4,16,128]{4,0,3,2,1:T(8,128)S(1)} %copy.5, f32[8,6,4,16,128]{4,0,3,2,1:T(8,128)} %copy-done.3, f32[6,4,16,128]{3,2,1,0:T(8,128)S(1)} %broadcast_multiply_fusion.2, f32[4,16,128]{2,1,0:T(8,128)S(1)} %get-tuple-element.45, ...), kind=kLoop, calls=%fused_computation.130 | loop fusion | flops 17252352 | bytes 11968608 | tf_op jit(solution)/shard_map/reduce_sum | solution.py:101
  81.7 0.8 fusion.54
  82.5 2.3 %fusion.55 = (f32[8,6,4,16,127]{4,0,3,2,1:T(8,128)}, f32[8,6,4,16,127]{4,0,3,2,1:T(8,128)}) fusion(f32[8,6,4,16,128]{4,0,3,2,1:T(8,128)S(1)} %get-tuple-element.10), kind=kLoop, calls=%fused_computation.135 | loop fusion | bytes 6242304 | tf_op jit(solution)/shard_map/slice | solution.py:37
  84.8 5.2 %collective-permute-start.8 = (f32[8,6,1,16,128]{4,0,3,2,1:T(8,128)}, f32[8,6,1,16,128]{4,0,3,2,1:T(8,128)S(1)}, u32[]{:S(2)}, u32[]{:S(2)}) collective-permute-start(f32[8,6,1,16,128]{4,0,3,2,1:T(8,128)} %get-tuple-element.26), channel_id=1, source_target_pairs={{4,0},{8,4},{12,8},{16,12},{20,16},{24,20},{28,24},{32,28},{36,32}... | collective-permute-start | bytes 1179656 | tf_op jit(solution)/shard_map/ppermute | solution.py:27
  90.0 1.9 collective-permute-start.9
  91.9 0.8 multiply_dynamic-update-slice_fusion.1
  92.8 0.7 subtract_dynamic-update-slice_fusion.1
  93.5 0.8 add_dynamic-update-slice_fusion.3
  94.3 0.8 add_dynamic-update-slice_fusion.2
  95.1 0.7 fusion.30
  95.9 0.7 collective-permute-done.8
  96.6 5.9 %collective-permute-done.9 = f32[8,6,1,16,128]{4,0,3,2,1:T(8,128)S(1)} collective-permute-done((f32[8,6,1,16,128]{4,0,3,2,1:T(8,128)S(1)}, f32[8,6,1,16,128]{4,0,3,2,1:T(8,128)S(1)}, u32[]{:S(2)}, u32[]{:S(2)}) %collective-permute-start.9) | collective-permute-done | bytes 393248 | tf_op jit(solution)/shard_map/ppermute | solution.py:25
  102.5 1.3 collective-permute-start.10
  103.8 3.0 %collective-permute-start.11 = (f32[8,6,6,1,128]{4,0,3,2,1:T(8,128)S(1)}, f32[8,6,6,1,128]{4,0,3,2,1:T(8,128)S(1)}, u32[]{:S(2)}, u32[]{:S(2)}) collective-permute-start(f32[8,6,6,1,128]{4,0,3,2,1:T(8,128)S(1)} %get-tuple-element.18), channel_id=1, source_target_pairs={{0,1},{1,2},{2,3},{4,5},{5,6},{6,7},{8,9},{9,10},{10,11},{12,13},{... | collective-permute-start | bytes 442376 | tf_op jit(solution)/shard_map/ppermute | solution.py:25
  106.8 33.3 %all-reduce.14.cloned.1.call-done = f32[6,4,16,128]{3,2,1,0:T(8,128)} async-done(((f32[6,4,16,128]{3,2,1,0:T(8,128)}), f32[6,4,16,128]{3,2,1,0:T(8,128)}) %all-reduce.14.cloned.1.call-update) | async-done | bytes 196624 | tf_op jit(solution)/shard_map/psum | solution.py:101
  140.2 0.9 broadcast_multiply_fusion.1
  141.2 0.6 copy-done.10
  141.8 0.1 copy-done.11
  141.9 6.5 %fusion.46 = (f32[6,4,16,128]{3,2,1,0:T(8,128)}, f32[8,6,4,16,128]{4,0,3,2,1:T(8,128)S(1)}) fusion(f32[8,6,4,16,128]{4,0,3,2,1:T(8,128)S(1)} %get-tuple-element.10, f32[8,6,4,16,128]{4,0,3,2,1:T(8,128)} %fusion.30, f32[6,4,16,128]{3,2,1,0:T(8,128)S(1)} %broadcast_multiply_fusion.1, f32[4,16,128]{2,1,0:T(8,128)S(1)} %get-tuple-element.45, ...), kind=kLoop, calls=%fused_computation.129 | loop fusion | flops 19218432 | bytes 11182176 | tf_op jit(solution)/shard_map/reduce_sum | solution.py:101
  148.4 0.9 fusion.53
  149.3 2.3 %fusion.52 = (f32[8,6,4,16,127]{4,0,3,2,1:T(8,128)}, f32[8,6,4,16,127]{4,0,3,2,1:T(8,128)}) fusion(f32[8,6,4,16,128]{4,0,3,2,1:T(8,128)S(1)} %get-tuple-element.6), kind=kLoop, calls=%fused_computation.132 | loop fusion | bytes 6242304 | tf_op jit(solution)/shard_map/slice | solution.py:37
  151.6 5.2 %collective-permute-start.12 = (f32[8,6,1,16,128]{4,0,3,2,1:T(8,128)}, f32[8,6,1,16,128]{4,0,3,2,1:T(8,128)}, u32[]{:S(2)}, u32[]{:S(2)}) collective-permute-start(f32[8,6,1,16,128]{4,0,3,2,1:T(8,128)} %get-tuple-element.24), channel_id=1, source_target_pairs={{4,0},{8,4},{12,8},{16,12},{20,16},{24,20},{28,24},{32,28},{36,32}... | collective-permute-start | bytes 1179656 | tf_op jit(solution)/shard_map/ppermute | solution.py:27
  156.8 1.9 collective-permute-start.13
  158.7 0.8 multiply_dynamic-update-slice_fusion
  159.5 0.7 subtract_dynamic-update-slice_fusion
  160.3 0.7 add_dynamic-update-slice_fusion.1
  161.0 0.8 add_dynamic-update-slice_fusion
  161.8 0.7 fusion.23
  162.5 0.8 collective-permute-done.12
  163.3 6.2 %collective-permute-done.13 = f32[8,6,1,16,128]{4,0,3,2,1:T(8,128)} collective-permute-done((f32[8,6,1,16,128]{4,0,3,2,1:T(8,128)}, f32[8,6,1,16,128]{4,0,3,2,1:T(8,128)}, u32[]{:S(2)}, u32[]{:S(2)}) %collective-permute-start.13) | collective-permute-done | bytes 393248 | tf_op jit(solution)/shard_map/ppermute | solution.py:25
  169.6 1.5 pad_maximum_fusion.22
  171.1 1.3 collective-permute-start.14
  172.4 3.7 %collective-permute-start.15 = (f32[8,6,6,1,128]{4,0,3,2,1:T(8,128)}, f32[8,6,6,1,128]{4,0,3,2,1:T(8,128)}, u32[]{:S(2)}, u32[]{:S(2)}) collective-permute-start(f32[8,6,6,1,128]{4,0,3,2,1:T(8,128)} %get-tuple-element.16), channel_id=1, source_target_pairs={{0,1},{1,2},{2,3},{4,5},{5,6},{6,7},{8,9},{9,10},{10,11},{12,13},{... | collective-permute-start | bytes 442376 | tf_op jit(solution)/shard_map/ppermute | solution.py:25
  176.1 30.8 %all-reduce.16.cloned.1.call-done = f32[6,4,16,128]{3,2,1,0:T(8,128)} async-done(((f32[6,4,16,128]{3,2,1,0:T(8,128)}), f32[6,4,16,128]{3,2,1,0:T(8,128)}) %all-reduce.16.cloned.1.call-update) | async-done | bytes 196624 | tf_op jit(solution)/shard_map/psum | solution.py:101
  206.9 0.9 broadcast_multiply_fusion
  207.9 5.1 %multiply_add_fusion = f32[8,6,4,16,128]{4,0,3,2,1:T(8,128)S(1)} fusion(f32[8,6,4,16,128]{4,0,3,2,1:T(8,128)S(1)} %get-tuple-element.6, f32[8,6,4,16,128]{4,0,3,2,1:T(8,128)} %fusion.23, f32[8,6,1,16,128]{4,0,3,2,1:T(8,128)} %collective-permute-done.12, f32[8,6,1,16,128]{4,0,3,2,1:T(8,128)} %collective-permute-done.13, ...), kind=kLoop, calls=%fused_computation.20 | loop fusion | flops 18874368 | bytes 10985568 | tf_op jit(solution)/shard_map/add | solution.py:105
  213.0 1.4 copy.24
  (50 shorter events, 0.6 us)
Async XLA Ops:
  6.5 67.4 %all-reduce.12.cloned.1.call-start = ((), (), s32[]{:S(2)}) async-start(), calls=%async_computation | async-start | bytes 393216 | tf_op jit(solution)/shard_map/psum | solution.py:101
  7.3 25.6 %collective-permute-start = (f32[4,1,16,128]{3,2,1,0:T(8,128)S(1)}, f32[4,1,16,128]{3,2,1,0:T(8,128)S(1)}, u32[]{:S(2)}, u32[]{:S(2)}) collective-permute-start(f32[4,1,16,128]{3,2,1,0:T(8,128)S(1)} %get-tuple-element.40), channel_id=1, source_target_pairs={{4,0},{8,4},{12,8},{16,12},{20,16},{24,20},{28,24},{32,28},{36,32}... | collective-permute-start | bytes 98312 | tf_op jit(solution)/shard_map/ppermute | solution.py:27
  15.0 18.0 %collective-permute-start.2 = (f32[4,1,16,128]{3,2,1,0:T(8,128)S(1)}, f32[4,1,16,128]{3,2,1,0:T(8,128)S(1)}, u32[]{:S(2)}, u32[]{:S(2)}) collective-permute-start(f32[4,1,16,128]{3,2,1,0:T(8,128)S(1)} %get-tuple-element.39), channel_id=1, source_target_pairs={{0,4},{4,8},{8,12},{12,16},{16,20},{20,24},{24,28},{28,32},{32,36}... | collective-permute-start | bytes 98312 | tf_op jit(solution)/shard_map/ppermute | solution.py:25
  19.2 8.9 %copy-start = (f32[8,6,4,16,128]{4,3,2,1,0:T(8,128)S(1)}, f32[8,6,4,16,128]{4,3,2,1,0:T(8,128)}, u32[]{:S(2)}) copy-start(f32[8,6,4,16,128]{4,3,2,1,0:T(8,128)} %param.4) | copy-start | bytes 4718596
  20.2 18.2 %collective-permute-start.3 = (f32[8,6,1,16,128]{4,0,3,2,1:T(8,128)}, f32[8,6,1,16,128]{4,0,3,2,1:T(8,128)}, u32[]{:S(2)}, u32[]{:S(2)}) collective-permute-start(f32[8,6,1,16,128]{4,0,3,2,1:T(8,128)} %get-tuple-element.30), channel_id=1, source_target_pairs={{0,4},{4,8},{8,12},{12,16},{16,20},{20,24},{24,28},{28,32},{32,36}... | collective-permute-start | bytes 1179656 | tf_op jit(solution)/shard_map/ppermute | solution.py:25
  22.1 18.2 %collective-permute-start.1 = (f32[8,6,1,16,128]{4,0,3,2,1:T(8,128)}, f32[8,6,1,16,128]{4,0,3,2,1:T(8,128)}, u32[]{:S(2)}, u32[]{:S(2)}) collective-permute-start(f32[8,6,1,16,128]{4,0,3,2,1:T(8,128)} %get-tuple-element.29), channel_id=1, source_target_pairs={{4,0},{8,4},{12,8},{16,12},{20,16},{24,20},{28,24},{32,28},{36,32}... | collective-permute-start | bytes 1179656 | tf_op jit(solution)/shard_map/ppermute | solution.py:27
  29.0 111.2 %all-reduce.14.cloned.1.call-start = ((), (), s32[]{:S(2)}) async-start(), calls=%async_computation.1 | async-start | bytes 393216 | tf_op jit(solution)/shard_map/psum | solution.py:101
  29.0 2.3 %copy-start.4 = (f32[4,16,128]{2,1,0:T(8,128)S(1)}, f32[4,16,128]{2,1,0:T(8,128)}, u32[]{:S(2)}) copy-start(f32[4,16,128]{2,1,0:T(8,128)} %param.6) | copy-start | bytes 98308
  31.5 0.7 copy-start.12
  31.5 1.5 copy-start.7
  32.2 8.1 %copy-start.3 = (f32[8,6,4,16,128]{4,0,3,2,1:T(8,128)}, f32[8,6,4,16,128]{4,0,3,2,1:T(8,128)S(1)}, u32[]{:S(2)}) copy-start(f32[8,6,4,16,128]{4,0,3,2,1:T(8,128)S(1)} %fusion.37) | copy-start | bytes 4718596
  33.0 5.1 %collective-permute-start.4 = (f32[4,6,1,128]{3,2,1,0:T(1,128)S(1)}, f32[4,6,1,128]{3,2,1,0:T(1,128)S(1)}, u32[]{:S(2)}, u32[]{:S(2)}) collective-permute-start(f32[4,6,1,128]{3,2,1,0:T(1,128)S(1)} %get-tuple-element.35), channel_id=1, source_target_pairs={{1,0},{2,1},{3,2},{5,4},{6,5},{7,6},{9,8},{10,9},{11,10},{13,12},{... | collective-permute-start | bytes 36872 | tf_op jit(solution)/shard_map/ppermute | solution.py:27
  34.3 3.9 %collective-permute-start.6 = (f32[4,6,1,128]{3,2,1,0:T(1,128)S(1)}, f32[4,6,1,128]{3,2,1,0:T(1,128)S(1)}, u32[]{:S(2)}, u32[]{:S(2)}) collective-permute-start(f32[4,6,1,128]{3,2,1,0:T(1,128)S(1)} %get-tuple-element.36), channel_id=1, source_target_pairs={{0,1},{1,2},{2,3},{4,5},{5,6},{6,7},{8,9},{9,10},{10,11},{12,13},{... | collective-permute-start | bytes 36872 | tf_op jit(solution)/shard_map/ppermute | solution.py:25
  41.3 1.4 copy-start.2
  42.8 32.1 %collective-permute-start.5 = (f32[8,6,6,1,128]{4,0,3,2,1:T(8,128)S(1)}, f32[8,6,6,1,128]{4,0,3,2,1:T(8,128)S(1)}, u32[]{:S(2)}, u32[]{:S(2)}) collective-permute-start(f32[8,6,6,1,128]{4,0,3,2,1:T(8,128)S(1)} %get-tuple-element.19), channel_id=1, source_target_pairs={{1,0},{2,1},{3,2},{5,4},{6,5},{7,6},{9,8},{10,9},{11,10},{13,12},{... | collective-permute-start | bytes 442376 | tf_op jit(solution)/shard_map/ppermute | solution.py:27
  44.1 30.8 %collective-permute-start.7 = (f32[8,6,6,1,128]{4,0,3,2,1:T(8,128)S(1)}, f32[8,6,6,1,128]{4,0,3,2,1:T(8,128)S(1)}, u32[]{:S(2)}, u32[]{:S(2)}) collective-permute-start(f32[8,6,6,1,128]{4,0,3,2,1:T(8,128)S(1)} %get-tuple-element.20), channel_id=1, source_target_pairs={{0,1},{1,2},{2,3},{4,5},{5,6},{6,7},{8,9},{9,10},{10,11},{12,13},{... | collective-permute-start | bytes 442376 | tf_op jit(solution)/shard_map/ppermute | solution.py:25
  74.9 0.7 copy-start.8
  74.9 0.7 copy-start.9
  84.8 11.8 %collective-permute-start.8 = (f32[8,6,1,16,128]{4,0,3,2,1:T(8,128)}, f32[8,6,1,16,128]{4,0,3,2,1:T(8,128)S(1)}, u32[]{:S(2)}, u32[]{:S(2)}) collective-permute-start(f32[8,6,1,16,128]{4,0,3,2,1:T(8,128)} %get-tuple-element.26), channel_id=1, source_target_pairs={{4,0},{8,4},{12,8},{16,12},{20,16},{24,20},{28,24},{32,28},{36,32}... | collective-permute-start | bytes 1179656 | tf_op jit(solution)/shard_map/ppermute | solution.py:27
  90.0 12.5 %collective-permute-start.9 = (f32[8,6,1,16,128]{4,0,3,2,1:T(8,128)S(1)}, f32[8,6,1,16,128]{4,0,3,2,1:T(8,128)S(1)}, u32[]{:S(2)}, u32[]{:S(2)}) collective-permute-start(f32[8,6,1,16,128]{4,0,3,2,1:T(8,128)S(1)} %get-tuple-element.25), channel_id=1, source_target_pairs={{0,4},{4,8},{8,12},{12,16},{16,20},{20,24},{24,28},{28,32},{32,36}... | collective-permute-start | bytes 1179656 | tf_op jit(solution)/shard_map/ppermute | solution.py:25
  94.3 112.6 %all-reduce.16.cloned.1.call-start = ((), (), s32[]{:S(2)}) async-start(), calls=%async_computation.2 | async-start | bytes 393216 | tf_op jit(solution)/shard_map/psum | solution.py:101
  96.6 44.6 %copy-start.5 = (f32[8,6,1,16,128]{4,0,3,2,1:T(8,128)}, f32[8,6,1,16,128]{4,0,3,2,1:T(8,128)S(1)}, u32[]{:S(2)}) copy-start(f32[8,6,1,16,128]{4,0,3,2,1:T(8,128)S(1)} %collective-permute-done.8) | copy-start | bytes 1179652
  102.5 38.7 %copy-start.6 = (f32[8,6,1,16,128]{4,0,3,2,1:T(8,128)}, f32[8,6,1,16,128]{4,0,3,2,1:T(8,128)S(1)}, u32[]{:S(2)}) copy-start(f32[8,6,1,16,128]{4,0,3,2,1:T(8,128)S(1)} %collective-permute-done.9) | copy-start | bytes 1179652
  102.5 38.6 %collective-permute-start.10 = (f32[8,6,6,1,128]{4,0,3,2,1:T(8,128)S(1)}, f32[8,6,6,1,128]{4,0,3,2,1:T(8,128)S(1)}, u32[]{:S(2)}, u32[]{:S(2)}) collective-permute-start(f32[8,6,6,1,128]{4,0,3,2,1:T(8,128)S(1)} %get-tuple-element.17), channel_id=1, source_target_pairs={{1,0},{2,1},{3,2},{5,4},{6,5},{7,6},{9,8},{10,9},{11,10},{13,12},{... | collective-permute-start | bytes 442376 | tf_op jit(solution)/shard_map/ppermute | solution.py:27
  103.8 37.4 %collective-permute-start.11 = (f32[8,6,6,1,128]{4,0,3,2,1:T(8,128)S(1)}, f32[8,6,6,1,128]{4,0,3,2,1:T(8,128)S(1)}, u32[]{:S(2)}, u32[]{:S(2)}) collective-permute-start(f32[8,6,6,1,128]{4,0,3,2,1:T(8,128)S(1)} %get-tuple-element.18), channel_id=1, source_target_pairs={{0,1},{1,2},{2,3},{4,5},{5,6},{6,7},{8,9},{9,10},{10,11},{12,13},{... | collective-permute-start | bytes 442376 | tf_op jit(solution)/shard_map/ppermute | solution.py:25
  141.2 0.6 copy-start.10
  141.2 0.7 copy-start.11
  151.6 11.8 %collective-permute-start.12 = (f32[8,6,1,16,128]{4,0,3,2,1:T(8,128)}, f32[8,6,1,16,128]{4,0,3,2,1:T(8,128)}, u32[]{:S(2)}, u32[]{:S(2)}) collective-permute-start(f32[8,6,1,16,128]{4,0,3,2,1:T(8,128)} %get-tuple-element.24), channel_id=1, source_target_pairs={{4,0},{8,4},{12,8},{16,12},{20,16},{24,20},{28,24},{32,28},{36,32}... | collective-permute-start | bytes 1179656 | tf_op jit(solution)/shard_map/ppermute | solution.py:27
  156.8 12.8 %collective-permute-start.13 = (f32[8,6,1,16,128]{4,0,3,2,1:T(8,128)}, f32[8,6,1,16,128]{4,0,3,2,1:T(8,128)}, u32[]{:S(2)}, u32[]{:S(2)}) collective-permute-start(f32[8,6,1,16,128]{4,0,3,2,1:T(8,128)} %get-tuple-element.23), channel_id=1, source_target_pairs={{0,4},{4,8},{8,12},{12,16},{16,20},{20,24},{24,28},{28,32},{32,36}... | collective-permute-start | bytes 1179656 | tf_op jit(solution)/shard_map/ppermute | solution.py:25
  162.5 45.4 %copy-start.1 = (f32[8,6,4,16,128]{4,3,2,1,0:T(8,128)S(1)}, f32[8,6,4,16,128]{4,3,2,1,0:T(8,128)}, u32[]{:S(2)}) copy-start(f32[8,6,4,16,128]{4,3,2,1,0:T(8,128)} %param.4) | copy-start | bytes 4718596
  171.1 36.8 %collective-permute-start.14 = (f32[8,6,6,1,128]{4,0,3,2,1:T(8,128)}, f32[8,6,6,1,128]{4,0,3,2,1:T(8,128)}, u32[]{:S(2)}, u32[]{:S(2)}) collective-permute-start(f32[8,6,6,1,128]{4,0,3,2,1:T(8,128)} %get-tuple-element.15), channel_id=1, source_target_pairs={{1,0},{2,1},{3,2},{5,4},{6,5},{7,6},{9,8},{10,9},{11,10},{13,12},{... | collective-permute-start | bytes 442376 | tf_op jit(solution)/shard_map/ppermute | solution.py:27
  172.4 35.5 %collective-permute-start.15 = (f32[8,6,6,1,128]{4,0,3,2,1:T(8,128)}, f32[8,6,6,1,128]{4,0,3,2,1:T(8,128)}, u32[]{:S(2)}, u32[]{:S(2)}) collective-permute-start(f32[8,6,6,1,128]{4,0,3,2,1:T(8,128)} %get-tuple-element.16), channel_id=1, source_target_pairs={{0,1},{1,2},{2,3},{4,5},{5,6},{6,7},{8,9},{9,10},{10,11},{12,13},{... | collective-permute-start | bytes 442376 | tf_op jit(solution)/shard_map/ppermute | solution.py:25
Sparse Core Ops, SparseCore 0:
  29.1 44.7 all-reduce.11
  94.4 45.7 all-reduce.13
  161.1 45.7 all-reduce.15
where the time goes:
time: 222 us; the launch traced here: 221 us
  waiting for transfers between devices  103 us (46%)
  starting transfers between devices  51.5 us (23%)
  other arithmetic  31.7 us (14%)
  local copies, waits for them, and re-layouts  21.2 us (10%)
  between operations  13.5 us (6%)
    psum x3, waiting for transfers between devices, advance(): field_sums = lax.psum(jnp.sum(section_now, axis=0), 'af')  89.3 us
    ppermute x8, starting transfers between devices, padded_2(): lax.ppermute(head, axis, [((i + 1) % count, i) for i in range(ends)])  29.2 us
    ppermute x8, starting transfers between devices, padded_2(): lax.ppermute(tail, axis, [(i, (i + 1) % count) for i in range(ends)])  22.2 us
    reduce_sum x3, other arithmetic, advance(): field_sums = lax.psum(jnp.sum(section_now, axis=0), 'af')  13.4 us
    ppermute x8, waiting for transfers between devices, padded_2(): lax.ppermute(tail, axis, [(i, (i + 1) % count) for i in range(ends)])  12.2 us
    unnamed x32, local copies, waits for them, and re-layouts  9.08 us
    slice x4, local copies, waits for them, and re-layouts, neighbours_z(): values[..., 1:]  6.84 us
    unnamed x12, other arithmetic  6.48 us
  transfers between devices with their start and end apart: 19, of which 8 were waited for; matrix products, arithmetic and copies ran while one was open for 11% of the time, Pallas kernels for 0%

commit v1 on v0

v1 whole, which is shorter than its diff:
```python
import functools

import jax
import jax.numpy as jnp
from jax import lax
from jax.experimental import pallas as pl
from jax.experimental.pallas import tpu as pltpu
from jax.sharding import PartitionSpec as P

MESH = pl.DeviceIdType.MESH
F32 = jnp.float32

FIELDS = 32
NS = 6
STEP = 0.3
MIX = 4.0
RADIATION = 0.5
NUCLEATION = (1.0, 0.8, 0.6, 0.5)
GROWTH = 0.5
OXIDATION = 0.3
WEIGHTS = ((0.0, 1.0), (0.75, 0.25), (1.0 / 3.0, 2.0 / 3.0))
EAST, WEST, NORTH, SOUTH, SUM1, SUM2 = range(6)


def sum_rows(tiles):
    row = lax.broadcasted_iota(jnp.int32, (8, 128), 0)
    low = row < 4
    quads = [
        jnp.where(low, tiles[i], tiles[i + 4])
        + pltpu.roll(jnp.where(low, tiles[i + 4], tiles[i]), 4, 0)
        for i in range(4)
    ]
    even = lax.rem(row, 4) < 2
    pairs = [
        jnp.where(even, quads[i], quads[i + 2])
        + jnp.where(even, pltpu.roll(quads[i], 6, 0), pltpu.roll(quads[i + 2], 2, 0))
        for i in range(2)
    ]
    first = lax.rem(row, 2) < 1
    return jnp.where(first, pairs[0], pairs[1]) + jnp.where(
        first, pltpu.roll(pairs[0], 7, 0), pltpu.roll(pairs[1], 1, 0)
    )


def spread(rows, i):
    return jnp.broadcast_to(rows[i : i + 1, :], (8, 128))


def kernel(
    counts,
    fields_hbm,
    velocity_hbm,
    diffusivity_hbm,
    wiener_hbm,
    out_hbm,
    rows_in,
    rows_out,
    p,
    coef,
    centre,
    weight,
    mean_row,
    part,
    part_1,
    half,
    part_2,
    speed_x,
    speed_y,
    speed_z,
    diffusion,
    wiener,
    in_sem,
    out_sem,
    own_sem,
    speed_send,
    speed_recv,
    send_sem,
    recv_sem,
):
    nx, ny, na = counts
    ax, ix, iy = lax.axis_index("af"), lax.axis_index("gx"), lax.axis_index("gy")
    has = {EAST: ix < nx - 1, WEST: ix > 0, NORTH: iy < ny - 1, SOUTH: iy > 0}
    back = {EAST: WEST, WEST: EAST, NORTH: SOUTH, SOUTH: NORTH}
    pair = {SUM1: ax + 1 - 2 * lax.rem(ax, 2), SUM2: na - 1 - ax}
    target = {
        EAST: {"gx": ix + 1},
        WEST: {"gx": ix - 1},
        NORTH: {"gy": iy + 1},
        SOUTH: {"gy": iy - 1},
        SUM1: {"af": pair[SUM1]},
        SUM2: {"af": pair[SUM2]},
    }

    def load_in(s):
        return pltpu.make_async_copy(fields_hbm.at[:, s], rows_in.at[s], in_sem.at[s])

    def store_out(s):
        return pltpu.make_async_copy(rows_out.at[s], out_hbm.at[:, s], out_sem.at[s])

    own = [
        pltpu.make_async_copy(velocity_hbm.at[0], speed_x.at[pl.ds(1, 4)], own_sem.at[0]),
        pltpu.make_async_copy(velocity_hbm.at[1], speed_y.at[:, pl.ds(8, 16)], own_sem.at[1]),
        pltpu.make_async_copy(velocity_hbm.at[2], speed_z, own_sem.at[2]),
        pltpu.make_async_copy(diffusivity_hbm, diffusion, own_sem.at[3]),
        pltpu.make_async_copy(wiener_hbm, wiener, own_sem.at[4]),
    ]

    def speed_face(way):
        src, dst = {
            EAST: (velocity_hbm.at[0, 3], speed_x.at[0]),
            WEST: (velocity_hbm.at[0, 0], speed_x.at[5]),
            NORTH: (velocity_hbm.at[1, :, pl.ds(8, 8)], speed_y.at[:, pl.ds(0, 8)]),
            SOUTH: (velocity_hbm.at[1, :, pl.ds(0, 8)], speed_y.at[:, pl.ds(24, 8)]),
        }[way]
        return pltpu.make_async_remote_copy(
            src_ref=src,
            dst_ref=dst,
            send_sem=speed_send.at[way],
            recv_sem=speed_recv.at[way],
            device_id=target[way],
            device_id_type=MESH,
        )

    def face(k, s, way):
        src, dst = {
            EAST: lambda: (p.at[k, s, 4, pl.ds(1, 16)], p.at[k, s, 0, pl.ds(1, 16)]),
            WEST: lambda: (p.at[k, s, 1, pl.ds(1, 16)], p.at[k, s, 5, pl.ds(1, 16)]),
            NORTH: lambda: (p.at[k, s, pl.ds(1, 4), 16], p.at[k, s, pl.ds(1, 4), 0]),
            SOUTH: lambda: (p.at[k, s, pl.ds(1, 4), 1], p.at[k, s, pl.ds(1, 4), 17]),
            SUM1: lambda: (part.at[k, s], part_1.at[k, s]),
            SUM2: lambda: (half.at[k, s], part_2.at[k, s]),
        }[way]()
        return pltpu.make_async_remote_copy(
            src_ref=src,
            dst_ref=dst,
            send_sem=send_sem.at[k, s, way],
            recv_sem=recv_sem.at[k, s, way],
            device_id=target[way],
            device_id_type=MESH,
        )

    def send(k, s, way):
        pl.when(has[way])(lambda: face(k, s, way).start())

    def arrived(k, s, way):
        pl.when(has[back[way]])(lambda: face(k, s, way).wait_recv())

    def blocks(first, step, count, body):
        def at(i, _):
            body(first + step * (i // 2), lax.rem(i, 2))
            return 0

        lax.fori_loop(0, 2 * count, at, 0)

    load_in(0).start()
    for copy in own:
        copy.start()
    for s in range(1, NS):
        load_in(s).start()

    barrier = pltpu.get_barrier_semaphore()
    expected = 2
    for way in (EAST, WEST, NORTH, SOUTH):
        pl.when(has[way])(
            lambda way=way: pl.semaphore_signal(
                barrier, inc=1, device_id=target[way], device_id_type=MESH
            )
        )
        expected = expected + has[way].astype(jnp.int32)
    for way in (SUM1, SUM2):
        pl.semaphore_signal(barrier, inc=1, device_id=target[way], device_id_type=MESH)

    zero = jnp.zeros((8, 128), F32)

    def clear_x(x, speed):
        def at(i, _):
            for y in range(16):
                p[i // NS, lax.rem(i, NS), x, 1 + y] = zero
            return 0

        lax.fori_loop(0, 3 * NS, at, 0)
        speed_x[speed] = jnp.zeros((16, 128), F32)

    def clear_y(y, speed):
        def at(i, _):
            for x in range(4):
                p[i // NS, lax.rem(i, NS), 1 + x, y] = zero
            return 0

        lax.fori_loop(0, 3 * NS, at, 0)
        for x in range(4):
            speed_y[x, speed : speed + 8] = zero

    pl.when(ix == 0)(lambda: clear_x(0, 0))
    pl.when(ix == nx - 1)(lambda: clear_x(5, 5))
    pl.when(iy == 0)(lambda: clear_y(0, 0))
    pl.when(iy == ny - 1)(lambda: clear_y(17, 24))

    pl.semaphore_wait(barrier, expected)

    def second_exchange(k, s):
        face(k, s, SUM1).wait_recv()
        half[k, s] = part[k, s] + part_1[k, s]
        face(k, s, SUM2).start()

    def mean_term(k, s):
        face(k, s, SUM2).wait_recv()
        mean_row[...] = (STEP * MIX / FIELDS) * diffusion[...] * (half[k, s] + part_2[k, s])

    def turn(s):
        flat = rows_in.reshape(NS * 8 * 64, 128)

        def body(x, h):
            tiles = []
            for i in range(8):
                start = s * 512 + x * 16 + h * 8 + i
                tiles.append(flat[pl.ds(start, 8, stride=64), :])
                p[0, s, x + 1, h * 8 + i + 1] = tiles[-1]
            part[0, s, x, pl.ds(h * 8, 8), :] = sum_rows(tiles)

        return body

    for s in range(NS):
        load_in(s).wait()
        blocks(0, 3, 2, turn(s))
        send(0, s, EAST)
        send(0, s, WEST)
        blocks(1, 1, 2, turn(s))
        send(0, s, NORTH)
        send(0, s, SOUTH)
        face(0, s, SUM1).start()
        if s == 0:
            for way in (EAST, WEST, NORTH, SOUTH):
                pl.when(has[way])(lambda way=way: speed_face(way).start())
        else:
            second_exchange(0, s - 1)

    for copy in own:
        copy.wait()
    for way in (EAST, WEST, NORTH, SOUTH):
        pl.when(has[back[way]])(lambda way=way: speed_face(way).wait_recv())

    draws = [jnp.broadcast_to(wiener[:, d : d + 1], (8, 128)) for d in range(3)]

    def coefficients(x, _):
        g = diffusion[x]
        diffuse = STEP * g
        stir = (0.5 * STEP) * jnp.sqrt((2.0 / STEP) * g)
        lane = lax.broadcasted_iota(jnp.int32, (16, 128), 1)
        upper, lower = lane < 127, lane > 0
        half_step = 0.5 * STEP
        base = [
            diffuse - half_step * speed_x[x + 2],
            diffuse + half_step * speed_x[x],
            diffuse - half_step * speed_y[x, 9:25, :],
            diffuse + half_step * speed_y[x, 7:23, :],
            jnp.where(upper, diffuse - half_step * pltpu.roll(speed_z[x], 127, 1), 0.0),
            jnp.where(lower, diffuse + half_step * pltpu.roll(speed_z[x], 1, 1), 0.0),
        ]
        stir_up, stir_down = jnp.where(upper, stir, 0.0), jnp.where(lower, stir, 0.0)
        keep = 1.0 - (6.0 + MIX) * diffuse
        for y in range(16):
            stir_y = spread(stir, y)
            for d in range(2):
                move = stir_y * draws[d]
                coef[2 * d, x, y] = spread(base[2 * d], y) + move
                coef[2 * d + 1, x, y] = spread(base[2 * d + 1], y) - move
            coef[4, x, y] = spread(base[4], y) + spread(stir_up, y) * draws[2]
            coef[5, x, y] = spread(base[5], y) - spread(stir_down, y) * draws[2]
            keep_y = spread(keep, y)
            centre[0, x, y] = keep_y
            centre[1, x, y] = keep_y - STEP * OXIDATION
        return 0

    lax.fori_loop(0, 4, coefficients, 0)

    def advance(k, s):
        base_weight, section_weight = WEIGHTS[k - 1]
        old = k - 1
        flat = rows_out.reshape(NS * 8 * 64, 128)

        def body(x, h):
            y0 = h * 8
            column = [p[old, s, x + 1, y0 + i] for i in range(10)]
            means = mean_row[x, pl.ds(y0, 8), :]
            tiles = []
            for i in range(8):
                y = y0 + i
                here = column[i + 1]
                new = (
                    centre[int(s >= 2), x, y] * here
                    + spread(means, i)
                    + coef[0, x, y] * p[old, s, x + 2, y + 1]
                    + coef[1, x, y] * p[old, s, x, y + 1]
                    + coef[2, x, y] * column[i + 2]
                    + coef[3, x, y] * column[i]
                    + coef[4, x, y] * pltpu.roll(here, 127, 1)
                    + coef[5, x, y] * pltpu.roll(here, 1, 1)
                )
                if s == 1:
                    mixture = p[old, 0, x + 1, y + 1]
                    square = mixture * mixture
                    w = square / (1.0 + square) / (1.0 + jnp.exp(-3.0 * here))
                    weight[x, y] = w
                    new = new - (STEP * RADIATION) * w
                elif s == 2:
                    new = new + (STEP * NUCLEATION[0]) * weight[x, y]
                elif s > 2:
                    new = new + weight[x, y] * (
                        STEP * NUCLEATION[s - 2] + (STEP * GROWTH) * p[old, s - 1, x + 1, y + 1]
                    )
                if base_weight:
                    new = base_weight * p[0, s, x + 1, y + 1] + section_weight * new
                tiles.append(new)
                if k < 3:
                    p[k, s, x + 1, y + 1] = new
                else:
                    flat[pl.ds(s * 512 + x * 16 + y, 8, stride=64), :] = new
            if k < 3:
                part[k, s, x, pl.ds(y0, 8), :] = sum_rows(tiles)

        return body

    for k in range(1, 4):
        for s in range(NS):
            if s == 0:
                second_exchange(k - 1, NS - 1)
            mean_term(k - 1, s)
            arrived(k - 1, s, NORTH)
            arrived(k - 1, s, SOUTH)
            blocks(1, 1, 2, advance(k, s))
            arrived(k - 1, s, EAST)
            arrived(k - 1, s, WEST)
            blocks(0, 3, 2, advance(k, s))
            if k < 3:
                for way in (EAST, WEST, NORTH, SOUTH):
                    send(k, s, way)
                face(k, s, SUM1).start()
                if s > 0:
                    second_exchange(k, s - 1)
            else:
                store_out(s).start()

    for way in (EAST, WEST, NORTH, SOUTH):
        pl.when(has[way])(lambda way=way: speed_face(way).wait_send())
        for k in range(3):
            for s in range(NS):
                pl.when(has[way])(lambda k=k, s=s, way=way: face(k, s, way).wait_send())
    for k in range(3):
        for s in range(NS):
            face(k, s, SUM1).wait_send()
            face(k, s, SUM2).wait_send()
    for s in range(NS):
        store_out(s).wait()


def local(fields_state, velocity, diffusivity, wiener_draw):
    counts = tuple(lax.axis_size(name) for name in ("gx", "gy", "af"))
    held = fields_state.shape
    dma = pltpu.SemaphoreType.DMA
    vmem = lambda *shape: pltpu.VMEM(shape, F32)
    out = pl.pallas_call(
        functools.partial(kernel, counts),
        out_shape=jax.ShapeDtypeStruct((8, NS, 64, 128), F32),
        in_specs=[pl.BlockSpec(memory_space=pl.ANY)] * 4,
        out_specs=pl.BlockSpec(memory_space=pl.ANY),
        scratch_shapes=[
            vmem(NS, 8, 64, 128),
            vmem(NS, 8, 64, 128),
            vmem(3, NS, 6, 18, 8, 128),
            vmem(6, 4, 16, 8, 128),
            vmem(2, 4, 16, 8, 128),
            vmem(4, 16, 8, 128),
            vmem(4, 16, 128),
            vmem(3, NS, 4, 16, 128),
            vmem(3, NS, 4, 16, 128),
            vmem(3, NS, 4, 16, 128),
            vmem(3, NS, 4, 16, 128),
            vmem(6, 16, 128),
            vmem(4, 32, 128),
            vmem(4, 16, 128),
            vmem(4, 16, 128),
            vmem(8, 3),
            dma((NS,)),
            dma((NS,)),
            dma((5,)),
            dma((4,)),
            dma((4,)),
            dma((3, NS, 6)),
            dma((3, NS, 6)),
        ],
        compiler_params=pltpu.CompilerParams(
            collective_id=0, has_side_effects=True, vmem_limit_bytes=48 * 1024 * 1024
        ),
    )(fields_state.reshape(8, NS, 64, 128), velocity, diffusivity, wiener_draw)
    return out.reshape(held)


def solution(mesh):
    return jax.shard_map(
        local,
        mesh=mesh,
        in_specs=(
            P("af", None, "gx", "gy", None),
            P(None, "gx", "gy", None),
            P("gx", "gy", None),
            P("af", None),
        ),
        out_specs=P("af", None, "gx", "gy", None),
        check_vma=False,
    )
```

time: 222 us -> 55 us (0.25)
  waiting for transfers between devices: 103 us -> 0 us
  starting transfers between devices: 51.5 us -> 0 us
  Pallas kernels: 0 us -> 49.5 us
  other arithmetic: 31.7 us -> 0 us
  local copies, waits for them, and re-layouts: 21.2 us -> 4.96 us
  between operations: 13.5 us -> 0.01 us
    psum x3 -> x0, waiting for transfers between devices: 89.3 us -> none  [advance(): field_sums = lax.psum(jnp.sum(section_now, axis=0), 'af')]
    ppermute x16 -> x0, starting transfers between devices: 51.4 us -> none  [the longest x8 29.2 us: padded_2(): lax.ppermute(head, axis, [((i + 1) % count, i) for i in range(ends)])]
    pallas_call x0 -> x1, Pallas kernels: none -> 49.5 us  [local(): pl.pallas_call(functools.partial(kernel, counts), out_shape=jax.ShapeDtyp...]
    ppermute x16 -> x0, waiting for transfers between devices: 13.8 us -> none  [the longest x8 12.2 us: padded_2(): lax.ppermute(tail, axis, [(i, (i + 1) % count) for i in range(ends)])]
    reduce_sum x3 -> x0, other arithmetic: 13.4 us -> none  [advance(): field_sums = lax.psum(jnp.sum(section_now, axis=0), 'af')]
    slice x8 -> x0, local copies, waits for them, and re-layouts: 9.54 us -> none  [the longest x4 6.84 us: neighbours_z(): values[..., 1:]]
    unnamed x12 -> x0, other arithmetic: 6.48 us -> none
    add x1 -> x0, other arithmetic: 5.06 us -> none  [advance(): weight_base * fields_state]
  transfers between devices with their start and end apart: 19 -> 0, of which waited for: 8 -> 0; matrix products, arithmetic and copies ran while one was open for 11% -> 0% of each run, Pallas kernels for 0% -> 0%
where the time goes in v1:
time: 55 us; the launch traced here: 54.4 us
  Pallas kernels  49.5 us (90%)
  local copies, waits for them, and re-layouts  4.96 us (9%)
    pallas_call x1, Pallas kernels, local(): pl.pallas_call(functools.partial(kernel, counts), out_shape=jax.ShapeDtyp...  49.5 us
    unnamed x8, local copies, waits for them, and re-layouts  4.96 us

profile of v1, /device:TPU:8, one launch (start us, length us, event | category | flops | bytes accessed | tf_op | source)
XLA Modules:
  0.0 54.4 jit_solution(4200258155600957350)
XLA Ops:
  0.0 0.8 %copy.5.wiener_hbm = f32[8,3]{1,0:T(8,128)S(1)} copy(f32[8,3]{0,1:T(4,128)} %param.7) | data formatting | bytes 192 | tf_op args[3]
  0.8 0.0 copy-start
  0.8 1.4 %copy-done = f32[8,6,4,16,128]{4,3,2,1,0:T(8,128)S(1)} copy-done((f32[8,6,4,16,128]{4,3,2,1,0:T(8,128)S(1)}, f32[8,6,4,16,128]{4,3,2,1,0:T(8,128)}, u32[]{:S(2)}) %copy-start) | copy-done | bytes 1572888
  2.2 0.0 copy-start.1
  2.2 0.9 %copy-done.1 = f32[3,4,16,128]{3,2,1,0:T(8,128)S(1)} copy-done((f32[3,4,16,128]{3,2,1,0:T(8,128)S(1)}, f32[3,4,16,128]{3,2,1,0:T(8,128)}, u32[]{:S(2)}) %copy-start.1) | copy-done | bytes 98328
  3.1 0.0 copy-start.2
  3.1 0.8 %copy-done.2 = f32[4,16,128]{2,1,0:T(8,128)S(1)} copy-done((f32[4,16,128]{2,1,0:T(8,128)S(1)}, f32[4,16,128]{2,1,0:T(8,128)}, u32[]{:S(2)}) %copy-start.2) | copy-done | bytes 32792
  3.8 49.5 %shard_map.46 = f32[8,6,64,128]{3,2,1,0:T(8,128)S(1)} custom-call(f32[8,6,64,128]{3,2,1,0:T(8,128)S(1)} %bitcast.3, f32[3,4,16,128]{3,2,1,0:T(8,128)S(1)} %copy-done.1, f32[4,16,128]{2,1,0:T(8,128)S(1)} %copy-done.2, f32[8,3]{1,0:T(8,128)S(1)} %copy.5.wiener_hbm), custom_call_target="tpu_custom_call" | custom-call | tf_op jit(solution)/shard_map/pallas_call | solution.py:362
  53.3 1.1 %copy.7 = f32[8,6,4,16,128]{4,3,2,1,0:T(8,128)} copy(f32[8,6,4,16,128]{4,3,2,1,0:T(8,128)S(1)} %bitcast.2) | data formatting | bytes 3145728
Async XLA Ops:
  0.8 1.4 %copy-start = (f32[8,6,4,16,128]{4,3,2,1,0:T(8,128)S(1)}, f32[8,6,4,16,128]{4,3,2,1,0:T(8,128)}, u32[]{:S(2)}) copy-start(f32[8,6,4,16,128]{4,3,2,1,0:T(8,128)} %param.4) | copy-start | bytes 4718596
  2.2 0.9 %copy-start.1 = (f32[3,4,16,128]{3,2,1,0:T(8,128)S(1)}, f32[3,4,16,128]{3,2,1,0:T(8,128)}, u32[]{:S(2)}) copy-start(f32[3,4,16,128]{3,2,1,0:T(8,128)} %velocity_hbm.1) | copy-start | bytes 294916
  3.1 0.8 %copy-start.2 = (f32[4,16,128]{2,1,0:T(8,128)S(1)}, f32[4,16,128]{2,1,0:T(8,128)}, u32[]{:S(2)}) copy-start(f32[4,16,128]{2,1,0:T(8,128)} %diffusivity_hbm.1) | copy-start | bytes 98308

commit v2 on v1

--- a/solution.py
+++ b/solution.py
@@ -12,6 +12,7 @@
 
 FIELDS = 32
 NS = 6
+PAIRS = 3
 STEP = 0.3
 MIX = 4.0
 RADIATION = 0.5
@@ -97,6 +98,9 @@
     def store_out(s):
         return pltpu.make_async_copy(rows_out.at[s], out_hbm.at[:, s], out_sem.at[s])
 
+    def two(c):
+        return pl.ds(2 * c, 2)
+
     own = [
         pltpu.make_async_copy(velocity_hbm.at[0], speed_x.at[pl.ds(1, 4)], own_sem.at[0]),
         pltpu.make_async_copy(velocity_hbm.at[1], speed_y.at[:, pl.ds(8, 16)], own_sem.at[1]),
@@ -121,7 +125,7 @@
             device_id_type=MESH,
         )
 
-    def face(k, s, way):
+    def face(k, s, way, recv=None):
         src, dst = {
             EAST: lambda: (p.at[k, s, 4, pl.ds(1, 16)], p.at[k, s, 0, pl.ds(1, 16)]),
             WEST: lambda: (p.at[k, s, 1, pl.ds(1, 16)], p.at[k, s, 5, pl.ds(1, 16)]),
@@ -133,17 +137,23 @@
         return pltpu.make_async_remote_copy(
             src_ref=src,
             dst_ref=dst,
-            send_sem=send_sem.at[k, s, way],
-            recv_sem=recv_sem.at[k, s, way],
+            send_sem=send_sem.at[way],
+            recv_sem=recv,
             device_id=target[way],
             device_id_type=MESH,
         )
 
-    def send(k, s, way):
-        pl.when(has[way])(lambda: face(k, s, way).start())
-
-    def arrived(k, s, way):
-        pl.when(has[back[way]])(lambda: face(k, s, way).wait_recv())
+    def chunk(k, c, way):
+        return face(k, two(c), way, recv_sem.at[k, c, way])
+
+    def all_sent(way):
+        face(pl.ds(0, 3), pl.ds(0, NS), way, recv_sem.at[0, 0, way]).wait_send()
+
+    def send(k, c, way):
+        pl.when(has[way])(lambda: chunk(k, c, way).start())
+
+    def arrived(k, c, way):
+        pl.when(has[back[way]])(lambda: chunk(k, c, way).wait_recv())
 
     def blocks(first, step, count, body):
         def at(i, _):
@@ -198,14 +208,16 @@
 
     pl.semaphore_wait(barrier, expected)
 
-    def second_exchange(k, s):
-        face(k, s, SUM1).wait_recv()
-        half[k, s] = part[k, s] + part_1[k, s]
-        face(k, s, SUM2).start()
-
-    def mean_term(k, s):
-        face(k, s, SUM2).wait_recv()
-        mean_row[...] = (STEP * MIX / FIELDS) * diffusion[...] * (half[k, s] + part_2[k, s])
+    def second_exchange(k, c):
+        chunk(k, c, SUM1).wait_recv()
+        half[k, two(c)] = part[k, two(c)] + part_1[k, two(c)]
+        chunk(k, c, SUM2).start()
+
+    def mean_term(k, c):
+        chunk(k, c, SUM2).wait_recv()
+        scale = (STEP * MIX / FIELDS) * diffusion[...]
+        for i in range(2):
+            mean_row[i] = scale * (half[k, 2 * c + i] + part_2[k, 2 * c + i])
 
     def turn(s):
         flat = rows_in.reshape(NS * 8 * 64, 128)
@@ -220,27 +232,36 @@
 
         return body
 
-    for s in range(NS):
-        load_in(s).wait()
-        blocks(0, 3, 2, turn(s))
-        send(0, s, EAST)
-        send(0, s, WEST)
-        blocks(1, 1, 2, turn(s))
-        send(0, s, NORTH)
-        send(0, s, SOUTH)
-        face(0, s, SUM1).start()
-        if s == 0:
+    for c in range(PAIRS):
+        for s in (2 * c, 2 * c + 1):
+            load_in(s).wait()
+            blocks(0, 3, 2, turn(s))
+        send(0, c, EAST)
+        send(0, c, WEST)
+        for s in (2 * c, 2 * c + 1):
+            blocks(1, 1, 2, turn(s))
+        send(0, c, NORTH)
+        send(0, c, SOUTH)
+        chunk(0, c, SUM1).start()
+        if c == 0:
             for way in (EAST, WEST, NORTH, SOUTH):
                 pl.when(has[way])(lambda way=way: speed_face(way).start())
         else:
-            second_exchange(0, s - 1)
+            second_exchange(0, c - 1)
 
     for copy in own:
         copy.wait()
     for way in (EAST, WEST, NORTH, SOUTH):
         pl.when(has[back[way]])(lambda way=way: speed_face(way).wait_recv())
 
-    draws = [jnp.broadcast_to(wiener[:, d : d + 1], (8, 128)) for d in range(3)]
+    diagonal = lax.broadcasted_iota(jnp.int32, (8, 8), 0) == lax.broadcasted_iota(
+        jnp.int32, (8, 8), 1
+    )
+    draws = []
+    for d in range(3):
+        row = jnp.broadcast_to(wiener[d : d + 1, :], (8, 8))
+        column = jnp.sum(jnp.where(diagonal, row, 0.0), axis=1, keepdims=True)
+        draws.append(jnp.broadcast_to(column, (8, 128)))
 
     def coefficients(x, _):
         g = diffusion[x]
@@ -274,82 +295,86 @@
 
     lax.fori_loop(0, 4, coefficients, 0)
 
-    def advance(k, s):
+    def advance(k, c):
         base_weight, section_weight = WEIGHTS[k - 1]
         old = k - 1
         flat = rows_out.reshape(NS * 8 * 64, 128)
 
         def body(x, h):
             y0 = h * 8
-            column = [p[old, s, x + 1, y0 + i] for i in range(10)]
-            means = mean_row[x, pl.ds(y0, 8), :]
-            tiles = []
+            tiles = [[], []]
+            columns = [[p[old, 2 * c + j, x + 1, y0 + i] for i in range(10)] for j in range(2)]
+            means = [mean_row[j, x, pl.ds(y0, 8), :] for j in range(2)]
             for i in range(8):
                 y = y0 + i
-                here = column[i + 1]
-                new = (
-                    centre[int(s >= 2), x, y] * here
-                    + spread(means, i)
-                    + coef[0, x, y] * p[old, s, x + 2, y + 1]
-                    + coef[1, x, y] * p[old, s, x, y + 1]
-                    + coef[2, x, y] * column[i + 2]
-                    + coef[3, x, y] * column[i]
-                    + coef[4, x, y] * pltpu.roll(here, 127, 1)
-                    + coef[5, x, y] * pltpu.roll(here, 1, 1)
-                )
-                if s == 1:
-                    mixture = p[old, 0, x + 1, y + 1]
-                    square = mixture * mixture
-                    w = square / (1.0 + square) / (1.0 + jnp.exp(-3.0 * here))
+                factor = [coef[d, x, y] for d in range(6)]
+                keep = centre[int(c > 0), x, y]
+                here = [columns[j][i + 1] for j in range(2)]
+                new = [
+                    keep * here[j]
+                    + spread(means[j], i)
+                    + factor[0] * p[old, 2 * c + j, x + 2, y + 1]
+                    + factor[1] * p[old, 2 * c + j, x, y + 1]
+                    + factor[2] * columns[j][i + 2]
+                    + factor[3] * columns[j][i]
+                    + factor[4] * pltpu.roll(here[j], 127, 1)
+                    + factor[5] * pltpu.roll(here[j], 1, 1)
+                    for j in range(2)
+                ]
+                if c == 0:
+                    square = here[0] * here[0]
+                    w = square / (1.0 + square) / (1.0 + jnp.exp(-3.0 * here[1]))
                     weight[x, y] = w
-                    new = new - (STEP * RADIATION) * w
-                elif s == 2:
-                    new = new + (STEP * NUCLEATION[0]) * weight[x, y]
-                elif s > 2:
-                    new = new + weight[x, y] * (
-                        STEP * NUCLEATION[s - 2] + (STEP * GROWTH) * p[old, s - 1, x + 1, y + 1]
-                    )
-                if base_weight:
-                    new = base_weight * p[0, s, x + 1, y + 1] + section_weight * new
-                tiles.append(new)
-                if k < 3:
-                    p[k, s, x + 1, y + 1] = new
+                    new[1] = new[1] - (STEP * RADIATION) * w
                 else:
-                    flat[pl.ds(s * 512 + x * 16 + y, 8, stride=64), :] = new
+                    w = weight[x, y]
+                    before = [p[old, 3, x + 1, y + 1] if c == 2 else None, here[0]]
+                    for j in range(2):
+                        gain = STEP * NUCLEATION[2 * c - 2 + j]
+                        if before[j] is not None:
+                            gain = gain + (STEP * GROWTH) * before[j]
+                        new[j] = new[j] + w * gain
+                for j in range(2):
+                    s = 2 * c + j
+                    if base_weight:
+                        new[j] = base_weight * p[0, s, x + 1, y + 1] + section_weight * new[j]
+                    tiles[j].append(new[j])
+                    if k < 3:
+                        p[k, s, x + 1, y + 1] = new[j]
+                    else:
+                        flat[pl.ds(s * 512 + x * 16 + y, 8, stride=64), :] = new[j]
             if k < 3:
-                part[k, s, x, pl.ds(y0, 8), :] = sum_rows(tiles)
+                for j in range(2):
+                    part[k, 2 * c + j, x, pl.ds(y0, 8), :] = sum_rows(tiles[j])
 
         return body
 
     for k in range(1, 4):
-        for s in range(NS):
-            if s == 0:
-                second_exchange(k - 1, NS - 1)
-            mean_term(k - 1, s)
-            arrived(k - 1, s, NORTH)
-            arrived(k - 1, s, SOUTH)
-            blocks(1, 1, 2, advance(k, s))
-            arrived(k - 1, s, EAST)
-            arrived(k - 1, s, WEST)
-            blocks(0, 3, 2, advance(k, s))
+        for c in range(PAIRS):
+            if c == 0:
+                second_exchange(k - 1, PAIRS - 1)
+            mean_term(k - 1, c)
+            arrived(k - 1, c, NORTH)
+            arrived(k - 1, c, SOUTH)
+            blocks(1, 1, 2, advance(k, c))
+            arrived(k - 1, c, EAST)
+            arrived(k - 1, c, WEST)
+            blocks(0, 3, 2, advance(k, c))
             if k < 3:
                 for way in (EAST, WEST, NORTH, SOUTH):
-                    send(k, s, way)
-                face(k, s, SUM1).start()
-                if s > 0:
-                    second_exchange(k, s - 1)
+                    send(k, c, way)
+                chunk(k, c, SUM1).start()
+                if c > 0:
+                    second_exchange(k, c - 1)
             else:
-                store_out(s).start()
+                store_out(2 * c).start()
+                store_out(2 * c + 1).start()
 
     for way in (EAST, WEST, NORTH, SOUTH):
         pl.when(has[way])(lambda way=way: speed_face(way).wait_send())
-        for k in range(3):
-            for s in range(NS):
-                pl.when(has[way])(lambda k=k, s=s, way=way: face(k, s, way).wait_send())
-    for k in range(3):
-        for s in range(NS):
-            face(k, s, SUM1).wait_send()
-            face(k, s, SUM2).wait_send()
+        pl.when(has[way])(lambda way=way: all_sent(way))
+    all_sent(SUM1)
+    all_sent(SUM2)
     for s in range(NS):
         store_out(s).wait()
 
@@ -371,7 +396,7 @@
             vmem(6, 4, 16, 8, 128),
             vmem(2, 4, 16, 8, 128),
             vmem(4, 16, 8, 128),
-            vmem(4, 16, 128),
+            vmem(2, 4, 16, 128),
             vmem(3, NS, 4, 16, 128),
             vmem(3, NS, 4, 16, 128),
             vmem(3, NS, 4, 16, 128),
@@ -380,19 +405,19 @@
             vmem(4, 32, 128),
             vmem(4, 16, 128),
             vmem(4, 16, 128),
-            vmem(8, 3),
+            vmem(3, 8),
             dma((NS,)),
             dma((NS,)),
             dma((5,)),
             dma((4,)),
             dma((4,)),
-            dma((3, NS, 6)),
-            dma((3, NS, 6)),
+            dma((6,)),
+            dma((3, PAIRS, 6)),
         ],
         compiler_params=pltpu.CompilerParams(
-            collective_id=0, has_side_effects=True, vmem_limit_bytes=48 * 1024 * 1024
+            collective_id=0, has_side_effects=True, vmem_limit_bytes=62 * 1024 * 1024
         ),
-    )(fields_state.reshape(8, NS, 64, 128), velocity, diffusivity, wiener_draw)
+    )(fields_state.reshape(8, NS, 64, 128), velocity, diffusivity, wiener_draw.T)
     return out.reshape(held)
 
 

time: 55 us -> 57.8 us (1.051)
  the two profiles are of different devices: /device:TPU:8 before, /device:TPU:16 now
where the time goes in v2:
time: 57.8 us; the launch traced here: 57.7 us
  Pallas kernels  55 us (95%)
  local copies, waits for them, and re-layouts  2.73 us (5%)
    pallas_call x1, Pallas kernels, local(): pl.pallas_call(functools.partial(kernel, counts), out_shape=jax.ShapeDtyp...  55 us
    unnamed x1, local copies, waits for them, and re-layouts  2.73 us

profile of v2, /device:TPU:16, one launch (start us, length us, event | category | flops | bytes accessed | tf_op | source)
XLA Modules:
  0.0 57.7 jit_solution(7209660726806824224)
XLA Ops:
  0.0 55.0 %shard_map.46 = f32[8,6,64,128]{3,2,1,0:T(8,128)} custom-call(f32[8,6,64,128]{3,2,1,0:T(8,128)} %bitcast.4, f32[3,4,16,128]{3,2,1,0:T(8,128)} %velocity_hbm.1, f32[4,16,128]{2,1,0:T(8,128)} %diffusivity_hbm.1, f32[3,8]{1,0:T(4,128)} %bitcast.5), custom_call_target="tpu_custom_call" | custom-call | tf_op jit(solution)/shard_map/pallas_call | solution.py:387
  55.0 2.7 %copy.6 = f32[8,6,4,16,128]{4,3,2,1,0:T(8,128)} copy(f32[8,6,4,16,128]{4,3,2,1,0:T(8,128)} %bitcast.3) | data formatting | bytes 3145728

commit v3 on v2

--- a/solution.py
+++ b/solution.py
@@ -53,9 +53,8 @@
     velocity_hbm,
     diffusivity_hbm,
     wiener_hbm,
-    out_hbm,
+    out,
     rows_in,
-    rows_out,
     p,
     coef,
     centre,
@@ -70,9 +69,11 @@
     speed_z,
     diffusion,
     wiener,
+    relay,
     in_sem,
-    out_sem,
     own_sem,
+    relay_send,
+    relay_recv,
     speed_send,
     speed_recv,
     send_sem,
@@ -92,11 +93,14 @@
         SUM2: {"af": pair[SUM2]},
     }
 
+    mid, end = nx // 2, nx - 1
+    to_relay = {EAST: ix == mid - 1, WEST: ix == mid}
+    is_relay = {EAST: ix == end, WEST: ix == 0}
+    relay_of = {EAST: {"gx": end}, WEST: {"gx": 0}}
+    relay_to = {EAST: {"gx": mid}, WEST: {"gx": mid - 1}}
+
     def load_in(s):
         return pltpu.make_async_copy(fields_hbm.at[:, s], rows_in.at[s], in_sem.at[s])
-
-    def store_out(s):
-        return pltpu.make_async_copy(rows_out.at[s], out_hbm.at[:, s], out_sem.at[s])
 
     def two(c):
         return pl.ds(2 * c, 2)
@@ -150,7 +154,50 @@
         face(pl.ds(0, 3), pl.ds(0, NS), way, recv_sem.at[0, 0, way]).wait_send()
 
     def send(k, c, way):
-        pl.when(has[way])(lambda: chunk(k, c, way).start())
+        if way not in to_relay:
+            pl.when(has[way])(lambda: chunk(k, c, way).start())
+            return
+
+        @pl.when(has[way] & jnp.logical_not(to_relay[way]))
+        def _():
+            chunk(k, c, way).start()
+
+        @pl.when(to_relay[way])
+        def _():
+            pltpu.make_async_remote_copy(
+                src_ref=p.at[k, 2 * c + 1, 4 if way == EAST else 1, pl.ds(1, 16)],
+                dst_ref=relay.at[k, c],
+                send_sem=send_sem.at[way],
+                recv_sem=relay_recv.at[k, c],
+                device_id=relay_of[way],
+                device_id_type=MESH,
+            ).start()
+            face(k, pl.ds(2 * c, 1), way, recv_sem.at[k, c, way]).start()
+
+    def passed_on(k, c, way):
+        return pltpu.make_async_remote_copy(
+            src_ref=relay.at[k, c],
+            dst_ref=p.at[k, 2 * c + 1, 0 if way == EAST else 5, pl.ds(1, 16)],
+            send_sem=relay_send,
+            recv_sem=recv_sem.at[k, c, way],
+            device_id=relay_to[way],
+            device_id_type=MESH,
+        )
+
+    def pass_on(k, c):
+        for way in (EAST, WEST):
+
+            @pl.when(is_relay[way])
+            def _():
+                pltpu.make_async_copy(relay.at[k, c], relay.at[k, c], relay_recv.at[k, c]).wait()
+                passed_on(k, c, way).start()
+
+    def all_passed_on():
+        for way in (EAST, WEST):
+
+            @pl.when(is_relay[way])
+            def _():
+                pltpu.make_async_copy(relay, relay, relay_send).wait()
 
     def arrived(k, c, way):
         pl.when(has[back[way]])(lambda: chunk(k, c, way).wait_recv())
@@ -177,6 +224,18 @@
             )
         )
         expected = expected + has[way].astype(jnp.int32)
+    for way in (EAST, WEST):
+        for near, partners in (
+            (to_relay[way], ({"gx": 0}, {"gx": end})),
+            (is_relay[way], ({"gx": mid - 1}, {"gx": mid})),
+        ):
+            expected = expected + 2 * near.astype(jnp.int32)
+
+            @pl.when(near)
+            def _(partners=partners):
+                for partner in partners:
+                    pl.semaphore_signal(barrier, inc=1, device_id=partner, device_id_type=MESH)
+
     for way in (SUM1, SUM2):
         pl.semaphore_signal(barrier, inc=1, device_id=target[way], device_id_type=MESH)
 
@@ -247,6 +306,7 @@
             for way in (EAST, WEST, NORTH, SOUTH):
                 pl.when(has[way])(lambda way=way: speed_face(way).start())
         else:
+            pass_on(0, c - 1)
             second_exchange(0, c - 1)
 
     for copy in own:
@@ -298,7 +358,7 @@
     def advance(k, c):
         base_weight, section_weight = WEIGHTS[k - 1]
         old = k - 1
-        flat = rows_out.reshape(NS * 8 * 64, 128)
+        flat = out.reshape(8 * NS * 64, 128)
 
         def body(x, h):
             y0 = h * 8
@@ -342,7 +402,7 @@
                     if k < 3:
                         p[k, s, x + 1, y + 1] = new[j]
                     else:
-                        flat[pl.ds(s * 512 + x * 16 + y, 8, stride=64), :] = new[j]
+                        flat[pl.ds(s * 64 + x * 16 + y, 8, stride=NS * 64), :] = new[j]
             if k < 3:
                 for j in range(2):
                     part[k, 2 * c + j, x, pl.ds(y0, 8), :] = sum_rows(tiles[j])
@@ -352,6 +412,7 @@
     for k in range(1, 4):
         for c in range(PAIRS):
             if c == 0:
+                pass_on(k - 1, PAIRS - 1)
                 second_exchange(k - 1, PAIRS - 1)
             mean_term(k - 1, c)
             arrived(k - 1, c, NORTH)
@@ -365,18 +426,15 @@
                     send(k, c, way)
                 chunk(k, c, SUM1).start()
                 if c > 0:
+                    pass_on(k, c - 1)
                     second_exchange(k, c - 1)
-            else:
-                store_out(2 * c).start()
-                store_out(2 * c + 1).start()
 
     for way in (EAST, WEST, NORTH, SOUTH):
         pl.when(has[way])(lambda way=way: speed_face(way).wait_send())
         pl.when(has[way])(lambda way=way: all_sent(way))
+    all_passed_on()
     all_sent(SUM1)
     all_sent(SUM2)
-    for s in range(NS):
-        store_out(s).wait()
 
 
 def local(fields_state, velocity, diffusivity, wiener_draw):
@@ -384,13 +442,13 @@
     held = fields_state.shape
     dma = pltpu.SemaphoreType.DMA
     vmem = lambda *shape: pltpu.VMEM(shape, F32)
+    held_in_hbm = (fields_state.reshape(8, NS, 64, 128), velocity, diffusivity, wiener_draw.T)
     out = pl.pallas_call(
         functools.partial(kernel, counts),
-        out_shape=jax.ShapeDtypeStruct((8, NS, 64, 128), F32),
-        in_specs=[pl.BlockSpec(memory_space=pl.ANY)] * 4,
-        out_specs=pl.BlockSpec(memory_space=pl.ANY),
+        out_shape=pltpu.VMEM((8, NS, 64, 128), F32),
+        in_specs=[pl.BlockSpec(memory_space=pltpu.HBM)] * 4,
+        out_specs=pl.BlockSpec(memory_space=pltpu.VMEM),
         scratch_shapes=[
-            vmem(NS, 8, 64, 128),
             vmem(NS, 8, 64, 128),
             vmem(3, NS, 6, 18, 8, 128),
             vmem(6, 4, 16, 8, 128),
@@ -406,18 +464,20 @@
             vmem(4, 16, 128),
             vmem(4, 16, 128),
             vmem(3, 8),
-            dma((NS,)),
+            vmem(3, PAIRS, 16, 8, 128),
             dma((NS,)),
             dma((5,)),
+            dma,
+            dma((3, PAIRS)),
             dma((4,)),
             dma((4,)),
             dma((6,)),
             dma((3, PAIRS, 6)),
         ],
         compiler_params=pltpu.CompilerParams(
-            collective_id=0, has_side_effects=True, vmem_limit_bytes=62 * 1024 * 1024
+            collective_id=0, has_side_effects=True, vmem_limit_bytes=48 * 1024 * 1024
         ),
-    )(fields_state.reshape(8, NS, 64, 128), velocity, diffusivity, wiener_draw.T)
+    )(*(pltpu.with_memory_space_constraint(x, pltpu.HBM) for x in held_in_hbm))
     return out.reshape(held)
 
 

time: 57.8 us -> 40.7 us (0.70)
  the two profiles are of different devices: /device:TPU:16 before, /device:TPU:8 now
where the time goes in v3:
time: 40.7 us; the launch traced here: 40.2 us
  Pallas kernels  39 us (96%)
  local copies, waits for them, and re-layouts  1.15 us (3%)
    pallas_call x1, Pallas kernels, local(): pl.pallas_call(functools.partial(kernel, counts), out_shape=pltpu.VMEM((8...  39 us
    unnamed x1, local copies, waits for them, and re-layouts  1.15 us

profile of v3, /device:TPU:8, one launch (start us, length us, event | category | flops | bytes accessed | tf_op | source)
XLA Modules:
  0.0 40.2 jit_solution(17364658382715624324)
XLA Ops:
  0.0 39.0 %shard_map.46 = f32[8,6,64,128]{3,2,1,0:T(8,128)S(1)} custom-call(f32[8,6,64,128]{3,2,1,0:T(8,128)} %bitcast.4, f32[3,4,16,128]{3,2,1,0:T(8,128)} %velocity_hbm.1, f32[4,16,128]{2,1,0:T(8,128)} %diffusivity_hbm.1, f32[3,8]{1,0:T(4,128)} %bitcast.5), custom_call_target="tpu_custom_call" | custom-call | tf_op jit(solution)/shard_map/pallas_call | solution.py:446
  39.0 1.1 %copy.6 = f32[8,6,4,16,128]{4,3,2,1,0:T(8,128)} copy(f32[8,6,4,16,128]{4,3,2,1,0:T(8,128)S(1)} %bitcast.3) | data formatting | bytes 3145728

commit v4 on v3

--- a/solution.py
+++ b/solution.py
@@ -282,11 +282,10 @@
         flat = rows_in.reshape(NS * 8 * 64, 128)
 
         def body(x, h):
-            tiles = []
+            start = s * 512 + x * 16 + h * 8
+            tiles = [flat[pl.ds(start + i, 8, stride=64), :] for i in range(8)]
             for i in range(8):
-                start = s * 512 + x * 16 + h * 8 + i
-                tiles.append(flat[pl.ds(start, 8, stride=64), :])
-                p[0, s, x + 1, h * 8 + i + 1] = tiles[-1]
+                p[0, s, x + 1, h * 8 + i + 1] = tiles[i]
             part[0, s, x, pl.ds(h * 8, 8), :] = sum_rows(tiles)
 
         return body
@@ -362,7 +361,7 @@
 
         def body(x, h):
             y0 = h * 8
-            tiles = [[], []]
+            tiles, weights = [[], []], []
             columns = [[p[old, 2 * c + j, x + 1, y0 + i] for i in range(10)] for j in range(2)]
             means = [mean_row[j, x, pl.ds(y0, 8), :] for j in range(2)]
             for i in range(8):
@@ -384,7 +383,7 @@
                 if c == 0:
                     square = here[0] * here[0]
                     w = square / (1.0 + square) / (1.0 + jnp.exp(-3.0 * here[1]))
-                    weight[x, y] = w
+                    weights.append(w)
                     new[1] = new[1] - (STEP * RADIATION) * w
                 else:
                     w = weight[x, y]
@@ -399,10 +398,15 @@
                     if base_weight:
                         new[j] = base_weight * p[0, s, x + 1, y + 1] + section_weight * new[j]
                     tiles[j].append(new[j])
+            for i, w in enumerate(weights):
+                weight[x, y0 + i] = w
+            for j in range(2):
+                s = 2 * c + j
+                for i in range(8):
                     if k < 3:
-                        p[k, s, x + 1, y + 1] = new[j]
+                        p[k, s, x + 1, y0 + i + 1] = tiles[j][i]
                     else:
-                        flat[pl.ds(s * 64 + x * 16 + y, 8, stride=NS * 64), :] = new[j]
+                        flat[pl.ds(s * 64 + x * 16 + y0 + i, 8, stride=NS * 64), :] = tiles[j][i]
             if k < 3:
                 for j in range(2):
                     part[k, 2 * c + j, x, pl.ds(y0, 8), :] = sum_rows(tiles[j])

time: 40.7 us -> 40.7 us (level)
  no operation moved by 1% of the time
where the time goes in v4:
time: 40.7 us; the launch traced here: 40.2 us
  Pallas kernels  39 us (96%)
  local copies, waits for them, and re-layouts  1.15 us (3%)
    pallas_call x1, Pallas kernels, local(): pl.pallas_call(functools.partial(kernel, counts), out_shape=pltpu.VMEM((8...  39 us
    unnamed x1, local copies, waits for them, and re-layouts  1.15 us

profile of v4, /device:TPU:8, one launch (start us, length us, event | category | flops | bytes accessed | tf_op | source)
XLA Modules:
  0.0 40.2 jit_solution(17364658382715624324)
XLA Ops:
  0.0 39.0 %shard_map.46 = f32[8,6,64,128]{3,2,1,0:T(8,128)S(1)} custom-call(f32[8,6,64,128]{3,2,1,0:T(8,128)} %bitcast.4, f32[3,4,16,128]{3,2,1,0:T(8,128)} %velocity_hbm.1, f32[4,16,128]{2,1,0:T(8,128)} %diffusivity_hbm.1, f32[3,8]{1,0:T(4,128)} %bitcast.5), custom_call_target="tpu_custom_call" | custom-call | tf_op jit(solution)/shard_map/pallas_call | solution.py:450
  39.0 1.1 %copy.6 = f32[8,6,4,16,128]{4,3,2,1,0:T(8,128)} copy(f32[8,6,4,16,128]{4,3,2,1,0:T(8,128)S(1)} %bitcast.3) | data formatting | bytes 3145728

commit v5 on v4

--- a/solution.py
+++ b/solution.py
@@ -74,6 +74,7 @@
     own_sem,
     relay_send,
     relay_recv,
+    x_sem,
     speed_send,
     speed_recv,
     send_sem,
@@ -129,10 +130,14 @@
             device_id_type=MESH,
         )
 
+    def face_x(k, s, way):
+        src, dst = {EAST: (4, 0), WEST: (1, 5)}[way]
+        return p.at[k, s, src, pl.ds(1, 16)], p.at[k, s, dst, pl.ds(1, 16)]
+
     def face(k, s, way, recv=None):
         src, dst = {
-            EAST: lambda: (p.at[k, s, 4, pl.ds(1, 16)], p.at[k, s, 0, pl.ds(1, 16)]),
-            WEST: lambda: (p.at[k, s, 1, pl.ds(1, 16)], p.at[k, s, 5, pl.ds(1, 16)]),
+            EAST: lambda: face_x(k, s, EAST),
+            WEST: lambda: face_x(k, s, WEST),
             NORTH: lambda: (p.at[k, s, pl.ds(1, 4), 16], p.at[k, s, pl.ds(1, 4), 0]),
             SOUTH: lambda: (p.at[k, s, pl.ds(1, 4), 1], p.at[k, s, pl.ds(1, 4), 17]),
             SUM1: lambda: (part.at[k, s], part_1.at[k, s]),
@@ -154,25 +159,34 @@
         face(pl.ds(0, 3), pl.ds(0, NS), way, recv_sem.at[0, 0, way]).wait_send()
 
     def send(k, c, way):
-        if way not in to_relay:
-            pl.when(has[way])(lambda: chunk(k, c, way).start())
-            return
-
-        @pl.when(has[way] & jnp.logical_not(to_relay[way]))
-        def _():
-            chunk(k, c, way).start()
-
-        @pl.when(to_relay[way])
-        def _():
-            pltpu.make_async_remote_copy(
-                src_ref=p.at[k, 2 * c + 1, 4 if way == EAST else 1, pl.ds(1, 16)],
-                dst_ref=relay.at[k, c],
-                send_sem=send_sem.at[way],
-                recv_sem=relay_recv.at[k, c],
-                device_id=relay_of[way],
-                device_id_type=MESH,
-            ).start()
-            face(k, pl.ds(2 * c, 1), way, recv_sem.at[k, c, way]).start()
+        pl.when(has[way])(lambda: chunk(k, c, way).start())
+
+    def x_face(k, s, way, by_relay=False):
+        src, dst = face_x(k, s, way)
+        return pltpu.make_async_remote_copy(
+            src_ref=src,
+            dst_ref=relay.at[k, s // 2] if by_relay else dst,
+            send_sem=x_sem.at[way, s % 2],
+            recv_sem=relay_recv.at[k, s // 2] if by_relay else recv_sem.at[k, s // 2, way],
+            device_id=relay_of[way] if by_relay else target[way],
+            device_id_type=MESH,
+        )
+
+    def left(k, s, way):
+        pl.when(has[way])(lambda: x_face(k, s, way).wait_send())
+
+    def send_x(k, c):
+        for s in (2 * c, 2 * c + 1):
+            for way in (EAST, WEST):
+                if k or c:
+                    left(k, s, way)
+                if s % 2 == 0:
+                    pl.when(has[way])(lambda: x_face(k, s, way).start())
+                else:
+                    pl.when(has[way] & jnp.logical_not(to_relay[way]))(
+                        lambda: x_face(k, s, way).start()
+                    )
+                    pl.when(to_relay[way])(lambda: x_face(k, s, way, by_relay=True).start())
 
     def passed_on(k, c, way):
         return pltpu.make_async_remote_copy(
@@ -294,8 +308,8 @@
         for s in (2 * c, 2 * c + 1):
             load_in(s).wait()
             blocks(0, 3, 2, turn(s))
-        send(0, c, EAST)
-        send(0, c, WEST)
+        if c == 0:
+            send_x(0, 0)
         for s in (2 * c, 2 * c + 1):
             blocks(1, 1, 2, turn(s))
         send(0, c, NORTH)
@@ -353,6 +367,8 @@
         return 0
 
     lax.fori_loop(0, 4, coefficients, 0)
+    for c in range(1, PAIRS):
+        send_x(0, c)
 
     def advance(k, c):
         base_weight, section_weight = WEIGHTS[k - 1]
@@ -426,16 +442,21 @@
             arrived(k - 1, c, WEST)
             blocks(0, 3, 2, advance(k, c))
             if k < 3:
-                for way in (EAST, WEST, NORTH, SOUTH):
+                for way in (NORTH, SOUTH):
                     send(k, c, way)
                 chunk(k, c, SUM1).start()
                 if c > 0:
                     pass_on(k, c - 1)
                     second_exchange(k, c - 1)
+                send_x(k, c)
 
     for way in (EAST, WEST, NORTH, SOUTH):
         pl.when(has[way])(lambda way=way: speed_face(way).wait_send())
-        pl.when(has[way])(lambda way=way: all_sent(way))
+        if way in to_relay:
+            left(2, NS - 2, way)
+            left(2, NS - 1, way)
+        else:
+            pl.when(has[way])(lambda way=way: all_sent(way))
     all_passed_on()
     all_sent(SUM1)
     all_sent(SUM2)
@@ -473,6 +494,7 @@
             dma((5,)),
             dma,
             dma((3, PAIRS)),
+            dma((2, 2)),
             dma((4,)),
             dma((4,)),
             dma((6,)),

time: 40.7 us -> 46.8 us (1.15)
  the two profiles are of different devices: /device:TPU:8 before, /device:TPU:16 now
where the time goes in v5:
time: 46.8 us; the launch traced here: 46.7 us
  Pallas kernels  45.6 us (97%)
  local copies, waits for them, and re-layouts  1.15 us (2%)
    pallas_call x1, Pallas kernels, local(): pl.pallas_call(functools.partial(kernel, counts), out_shape=pltpu.VMEM((8...  45.6 us
    unnamed x1, local copies, waits for them, and re-layouts  1.15 us

profile of v5, /device:TPU:16, one launch (start us, length us, event | category | flops | bytes accessed | tf_op | source)
XLA Modules:
  0.0 46.7 jit_solution(2975129771834527076)
XLA Ops:
  0.0 45.6 %shard_map.46 = f32[8,6,64,128]{3,2,1,0:T(8,128)S(1)} custom-call(f32[8,6,64,128]{3,2,1,0:T(8,128)} %bitcast.4, f32[3,4,16,128]{3,2,1,0:T(8,128)} %velocity_hbm.1, f32[4,16,128]{2,1,0:T(8,128)} %diffusivity_hbm.1, f32[3,8]{1,0:T(4,128)} %bitcast.5), custom_call_target="tpu_custom_call" | custom-call | tf_op jit(solution)/shard_map/pallas_call | solution.py:471
  45.6 1.1 %copy.6 = f32[8,6,4,16,128]{4,3,2,1,0:T(8,128)} copy(f32[8,6,4,16,128]{4,3,2,1,0:T(8,128)S(1)} %bitcast.3) | data formatting | bytes 3145728

commit v6 on v4

--- a/solution.py
+++ b/solution.py
@@ -19,7 +19,6 @@
 NUCLEATION = (1.0, 0.8, 0.6, 0.5)
 GROWTH = 0.5
 OXIDATION = 0.3
-WEIGHTS = ((0.0, 1.0), (0.75, 0.25), (1.0 / 3.0, 2.0 / 3.0))
 EAST, WEST, NORTH, SOUTH, SUM1, SUM2 = range(6)
 
 
@@ -202,12 +201,8 @@
     def arrived(k, c, way):
         pl.when(has[back[way]])(lambda: chunk(k, c, way).wait_recv())
 
-    def blocks(first, step, count, body):
-        def at(i, _):
-            body(first + step * (i // 2), lax.rem(i, 2))
-            return 0
-
-        lax.fori_loop(0, 2 * count, at, 0)
+    def blocks(count, body):
+        lax.fori_loop(0, count, lambda i, _: (body(i), 0)[1], 0)
 
     load_in(0).start()
     for copy in own:
@@ -278,35 +273,43 @@
         for i in range(2):
             mean_row[i] = scale * (half[k, 2 * c + i] + part_2[k, 2 * c + i])
 
-    def turn(s):
-        flat = rows_in.reshape(NS * 8 * 64, 128)
-
-        def body(x, h):
+    flat_in = rows_in.reshape(NS * 8 * 64, 128)
+
+    def turn(c, planes):
+        def body(i):
+            s, x, h = 2 * c + i // 4, planes(lax.rem(i // 2, 2)), lax.rem(i, 2)
             start = s * 512 + x * 16 + h * 8
-            tiles = [flat[pl.ds(start + i, 8, stride=64), :] for i in range(8)]
-            for i in range(8):
-                p[0, s, x + 1, h * 8 + i + 1] = tiles[i]
+            tiles = [flat_in[pl.ds(start + y, 8, stride=64), :] for y in range(8)]
+            for y in range(8):
+                p[0, s, x + 1, h * 8 + y + 1] = tiles[y]
             part[0, s, x, pl.ds(h * 8, 8), :] = sum_rows(tiles)
 
         return body
 
-    for c in range(PAIRS):
-        for s in (2 * c, 2 * c + 1):
-            load_in(s).wait()
-            blocks(0, 3, 2, turn(s))
+    def section_0(c, _):
+        load_in(2 * c).wait()
+        load_in(2 * c + 1).wait()
+        blocks(8, turn(c, lambda i: 3 * i))
         send(0, c, EAST)
         send(0, c, WEST)
-        for s in (2 * c, 2 * c + 1):
-            blocks(1, 1, 2, turn(s))
+        blocks(8, turn(c, lambda i: 1 + i))
         send(0, c, NORTH)
         send(0, c, SOUTH)
         chunk(0, c, SUM1).start()
-        if c == 0:
+
+        @pl.when(c == 0)
+        def _():
             for way in (EAST, WEST, NORTH, SOUTH):
                 pl.when(has[way])(lambda way=way: speed_face(way).start())
-        else:
+
+        @pl.when(c > 0)
+        def _():
             pass_on(0, c - 1)
             second_exchange(0, c - 1)
+
+        return 0
+
+    lax.fori_loop(0, PAIRS, section_0, 0)
 
     for copy in own:
         copy.wait()
@@ -354,13 +357,21 @@
 
     lax.fori_loop(0, 4, coefficients, 0)
 
+    flat_out = out.reshape(8 * NS * 64, 128)
+
     def advance(k, c):
-        base_weight, section_weight = WEIGHTS[k - 1]
         old = k - 1
-        flat = out.reshape(8 * NS * 64, 128)
-
-        def body(x, h):
-            y0 = h * 8
+        base_weight = jnp.where(k == 1, 0.0, jnp.where(k == 2, 0.75, 1.0 / 3.0))
+        section_weight = jnp.where(k == 1, 1.0, jnp.where(k == 2, 0.25, 2.0 / 3.0))
+
+        def body(turn):
+            x, y0 = jnp.where(turn < 4, 1 + turn // 2, 3 * (turn // 2) - 6), 8 * lax.rem(turn, 2)
+
+            @pl.when(turn == 4)
+            def _():
+                arrived(old, c, EAST)
+                arrived(old, c, WEST)
+
             tiles, weights = [[], []], []
             columns = [[p[old, 2 * c + j, x + 1, y0 + i] for i in range(10)] for j in range(2)]
             means = [mean_row[j, x, pl.ds(y0, 8), :] for j in range(2)]
@@ -394,44 +405,48 @@
                             gain = gain + (STEP * GROWTH) * before[j]
                         new[j] = new[j] + w * gain
                 for j in range(2):
-                    s = 2 * c + j
-                    if base_weight:
-                        new[j] = base_weight * p[0, s, x + 1, y + 1] + section_weight * new[j]
-                    tiles[j].append(new[j])
+                    start = p[0, 2 * c + j, x + 1, y + 1]
+                    tiles[j].append(base_weight * start + section_weight * new[j])
             for i, w in enumerate(weights):
                 weight[x, y0 + i] = w
-            for j in range(2):
-                s = 2 * c + j
-                for i in range(8):
-                    if k < 3:
-                        p[k, s, x + 1, y0 + i + 1] = tiles[j][i]
-                    else:
-                        flat[pl.ds(s * 64 + x * 16 + y0 + i, 8, stride=NS * 64), :] = tiles[j][i]
-            if k < 3:
+
+            @pl.when(k < 3)
+            def _():
                 for j in range(2):
+                    for i in range(8):
+                        p[k, 2 * c + j, x + 1, y0 + i + 1] = tiles[j][i]
                     part[k, 2 * c + j, x, pl.ds(y0, 8), :] = sum_rows(tiles[j])
 
+            @pl.when(k == 3)
+            def _():
+                for j in range(2):
+                    row = (2 * c + j) * 64 + x * 16 + y0
+                    for i in range(8):
+                        flat_out[pl.ds(row + i, 8, stride=NS * 64), :] = tiles[j][i]
+
         return body
 
-    for k in range(1, 4):
+    def section(k, _):
+        pass_on(k - 1, PAIRS - 1)
+        second_exchange(k - 1, PAIRS - 1)
         for c in range(PAIRS):
-            if c == 0:
-                pass_on(k - 1, PAIRS - 1)
-                second_exchange(k - 1, PAIRS - 1)
             mean_term(k - 1, c)
             arrived(k - 1, c, NORTH)
             arrived(k - 1, c, SOUTH)
-            blocks(1, 1, 2, advance(k, c))
-            arrived(k - 1, c, EAST)
-            arrived(k - 1, c, WEST)
-            blocks(0, 3, 2, advance(k, c))
-            if k < 3:
+            blocks(8, advance(k, c))
+
+            @pl.when(k < 3)
+            def _():
                 for way in (EAST, WEST, NORTH, SOUTH):
                     send(k, c, way)
                 chunk(k, c, SUM1).start()
                 if c > 0:
                     pass_on(k, c - 1)
                     second_exchange(k, c - 1)
+
+        return 0
+
+    lax.fori_loop(1, 4, section, 0)
 
     for way in (EAST, WEST, NORTH, SOUTH):
         pl.when(has[way])(lambda way=way: speed_face(way).wait_send())

time: 40.7 us -> 41.7 us (1.025)
  Pallas kernels: 39 us -> 40 us
    pallas_call x1, Pallas kernels: 39 us -> 40 us  [local(): pl.pallas_call(functools.partial(kernel, counts), out_shape=pltpu.VMEM((8...]
where the time goes in v6:
time: 41.7 us; the launch traced here: 41.2 us
  Pallas kernels  40 us (96%)
  local copies, waits for them, and re-layouts  1.15 us (3%)
    pallas_call x1, Pallas kernels, local(): pl.pallas_call(functools.partial(kernel, counts), out_shape=pltpu.VMEM((8...  40 us
    unnamed x1, local copies, waits for them, and re-layouts  1.15 us

profile of v6, /device:TPU:8, one launch (start us, length us, event | category | flops | bytes accessed | tf_op | source)
XLA Modules:
  0.0 41.2 jit_solution(7960643173396072101)
XLA Ops:
  0.0 40.0 %shard_map.46 = f32[8,6,64,128]{3,2,1,0:T(8,128)S(1)} custom-call(f32[8,6,64,128]{3,2,1,0:T(8,128)} %bitcast.4, f32[3,4,16,128]{3,2,1,0:T(8,128)} %velocity_hbm.1, f32[4,16,128]{2,1,0:T(8,128)} %diffusivity_hbm.1, f32[3,8]{1,0:T(4,128)} %bitcast.5), custom_call_target="tpu_custom_call" | custom-call | tf_op jit(solution)/shard_map/pallas_call | solution.py:465
  40.0 1.1 %copy.6 = f32[8,6,4,16,128]{4,3,2,1,0:T(8,128)} copy(f32[8,6,4,16,128]{4,3,2,1,0:T(8,128)S(1)} %bitcast.3) | data formatting | bytes 3145728

commit v7 on v4

--- a/solution.py
+++ b/solution.py
@@ -70,6 +70,8 @@
     diffusion,
     wiener,
     relay,
+    raw,
+    raw_relay,
     in_sem,
     own_sem,
     relay_send,
@@ -131,8 +133,6 @@
 
     def face(k, s, way, recv=None):
         src, dst = {
-            EAST: lambda: (p.at[k, s, 4, pl.ds(1, 16)], p.at[k, s, 0, pl.ds(1, 16)]),
-            WEST: lambda: (p.at[k, s, 1, pl.ds(1, 16)], p.at[k, s, 5, pl.ds(1, 16)]),
             NORTH: lambda: (p.at[k, s, pl.ds(1, 4), 16], p.at[k, s, pl.ds(1, 4), 0]),
             SOUTH: lambda: (p.at[k, s, pl.ds(1, 4), 1], p.at[k, s, pl.ds(1, 4), 17]),
             SUM1: lambda: (part.at[k, s], part_1.at[k, s]),
@@ -151,46 +151,77 @@
         return face(k, two(c), way, recv_sem.at[k, c, way])
 
     def all_sent(way):
-        face(pl.ds(0, 3), pl.ds(0, NS), way, recv_sem.at[0, 0, way]).wait_send()
-
-    def send(k, c, way):
-        if way not in to_relay:
-            pl.when(has[way])(lambda: chunk(k, c, way).start())
-            return
-
-        @pl.when(has[way] & jnp.logical_not(to_relay[way]))
-        def _():
-            chunk(k, c, way).start()
-
-        @pl.when(to_relay[way])
-        def _():
-            pltpu.make_async_remote_copy(
-                src_ref=p.at[k, 2 * c + 1, 4 if way == EAST else 1, pl.ds(1, 16)],
-                dst_ref=relay.at[k, c],
-                send_sem=send_sem.at[way],
-                recv_sem=relay_recv.at[k, c],
-                device_id=relay_of[way],
-                device_id_type=MESH,
-            ).start()
-            face(k, pl.ds(2 * c, 1), way, recv_sem.at[k, c, way]).start()
-
-    def passed_on(k, c, way):
+        if way in to_relay:
+            all_x = p.at[:, :, 1, pl.ds(1, 16)]
+            copy_x((all_x, all_x), way, recv_sem.at[0, 0, way], target[way]).wait_send()
+        else:
+            face(pl.ds(0, 3), pl.ds(0, NS), way, recv_sem.at[0, 0, way]).wait_send()
+
+    def x_face(k, c, way, s=None):
+        src, dst = {EAST: (4, 0), WEST: (1, 5)}[way]
+        side = way
+        which = pl.ds(2 * c, 2) if s is None else pl.ds(2 * c + s, 1)
+        to = pl.ds(0, 2) if s is None else pl.ds(s, 1)
+        if k == 0:
+            refs = fields_hbm.at[:, which, pl.ds(16 * (src - 1), 16)], raw.at[side, c, :, to]
+        else:
+            refs = p.at[k, which, src, pl.ds(1, 16)], p.at[k, which, dst, pl.ds(1, 16)]
+        return refs
+
+    def copy_x(refs, way, recv, to):
         return pltpu.make_async_remote_copy(
-            src_ref=relay.at[k, c],
-            dst_ref=p.at[k, 2 * c + 1, 0 if way == EAST else 5, pl.ds(1, 16)],
-            send_sem=relay_send,
-            recv_sem=recv_sem.at[k, c, way],
-            device_id=relay_to[way],
+            src_ref=refs[0],
+            dst_ref=refs[1],
+            send_sem=send_sem.at[way],
+            recv_sem=recv,
+            device_id=to,
             device_id_type=MESH,
         )
 
+    def relay_at(k, c):
+        return raw_relay.at[c] if k == 0 else relay.at[k - 1, c]
+
+    def send_x(k, c):
+        for way in (EAST, WEST):
+            recv = recv_sem.at[k, c, way]
+
+            @pl.when(has[way] & jnp.logical_not(to_relay[way]))
+            def _():
+                copy_x(x_face(k, c, way), way, recv, target[way]).start()
+
+            @pl.when(to_relay[way])
+            def _():
+                src = x_face(k, c, way, 1)[0]
+                copy_x(
+                    (src, relay_at(k, c)), way, relay_recv.at[k, c], relay_of[way]
+                ).start()
+                copy_x(x_face(k, c, way, 0), way, recv, target[way]).start()
+
+    def send(k, c, way):
+        pl.when(has[way])(lambda: chunk(k, c, way).start())
+
+    def arrived_x(k, c):
+        for way in (EAST, WEST):
+
+            @pl.when(has[back[way]])
+            def _():
+                copy_x(x_face(k, c, way), way, recv_sem.at[k, c, way], target[way]).wait_recv()
+
     def pass_on(k, c):
         for way in (EAST, WEST):
 
             @pl.when(is_relay[way])
             def _():
-                pltpu.make_async_copy(relay.at[k, c], relay.at[k, c], relay_recv.at[k, c]).wait()
-                passed_on(k, c, way).start()
+                here = relay_at(k, c)
+                pltpu.make_async_copy(here, here, relay_recv.at[k, c]).wait()
+                pltpu.make_async_remote_copy(
+                    src_ref=here,
+                    dst_ref=x_face(k, c, way, 1)[1],
+                    send_sem=relay_send,
+                    recv_sem=recv_sem.at[k, c, way],
+                    device_id=relay_to[way],
+                    device_id_type=MESH,
+                ).start()
 
     def all_passed_on():
         for way in (EAST, WEST):
@@ -198,6 +229,7 @@
             @pl.when(is_relay[way])
             def _():
                 pltpu.make_async_copy(relay, relay, relay_send).wait()
+                pltpu.make_async_copy(raw_relay, raw_relay, relay_send).wait()
 
     def arrived(k, c, way):
         pl.when(has[back[way]])(lambda: chunk(k, c, way).wait_recv())
@@ -266,6 +298,11 @@
     pl.when(iy == ny - 1)(lambda: clear_y(17, 24))
 
     pl.semaphore_wait(barrier, expected)
+    send_x(0, 0)
+    for way in (EAST, WEST, NORTH, SOUTH):
+        pl.when(has[way])(lambda way=way: speed_face(way).start())
+    for c in range(1, PAIRS):
+        send_x(0, c)
 
     def second_exchange(k, c):
         chunk(k, c, SUM1).wait_recv()
@@ -290,21 +327,27 @@
 
         return body
 
+    raw_rows = raw.reshape(2 * PAIRS * 8 * 32, 128)
+
+    def turn_face(c, way):
+        def at(i, _):
+            j, h = i // 2, lax.rem(i, 2)
+            start = (way * PAIRS + c) * 256 + i * 8
+            tiles = [raw_rows[pl.ds(start + y, 8, stride=32), :] for y in range(8)]
+            for y in range(8):
+                p[0, 2 * c + j, 0 if way == EAST else 5, h * 8 + y + 1] = tiles[y]
+            return 0
+
+        lax.fori_loop(0, 4, at, 0)
+
     for c in range(PAIRS):
         for s in (2 * c, 2 * c + 1):
             load_in(s).wait()
-            blocks(0, 3, 2, turn(s))
-        send(0, c, EAST)
-        send(0, c, WEST)
-        for s in (2 * c, 2 * c + 1):
-            blocks(1, 1, 2, turn(s))
+            blocks(0, 1, 4, turn(s))
         send(0, c, NORTH)
         send(0, c, SOUTH)
         chunk(0, c, SUM1).start()
-        if c == 0:
-            for way in (EAST, WEST, NORTH, SOUTH):
-                pl.when(has[way])(lambda way=way: speed_face(way).start())
-        else:
+        if c > 0:
             pass_on(0, c - 1)
             second_exchange(0, c - 1)
 
@@ -415,23 +458,26 @@
 
     for k in range(1, 4):
         for c in range(PAIRS):
-            if c == 0:
-                pass_on(k - 1, PAIRS - 1)
-                second_exchange(k - 1, PAIRS - 1)
             mean_term(k - 1, c)
             arrived(k - 1, c, NORTH)
             arrived(k - 1, c, SOUTH)
             blocks(1, 1, 2, advance(k, c))
-            arrived(k - 1, c, EAST)
-            arrived(k - 1, c, WEST)
+            arrived_x(k - 1, c)
+            if k == 1:
+                for way in (EAST, WEST):
+                    pl.when(has[back[way]])(lambda way=way: turn_face(c, way))
             blocks(0, 3, 2, advance(k, c))
             if k < 3:
-                for way in (EAST, WEST, NORTH, SOUTH):
+                send_x(k, c)
+                for way in (NORTH, SOUTH):
                     send(k, c, way)
                 chunk(k, c, SUM1).start()
-                if c > 0:
-                    pass_on(k, c - 1)
-                    second_exchange(k, c - 1)
+            if c == 0:
+                pass_on(k - 1, PAIRS - 1)
+                second_exchange(k - 1, PAIRS - 1)
+            elif k < 3:
+                pass_on(k, c - 1)
+                second_exchange(k, c - 1)
 
     for way in (EAST, WEST, NORTH, SOUTH):
         pl.when(has[way])(lambda way=way: speed_face(way).wait_send())
@@ -468,7 +514,9 @@
             vmem(4, 16, 128),
             vmem(4, 16, 128),
             vmem(3, 8),
-            vmem(3, PAIRS, 16, 8, 128),
+            vmem(2, PAIRS, 1, 16, 8, 128),
+            vmem(2, PAIRS, 8, 2, 16, 128),
+            vmem(PAIRS, 8, 1, 16, 128),
             dma((NS,)),
             dma((5,)),
             dma,

time: 40.7 us -> 40.5 us (level)
  no operation moved by 1% of the time
where the time goes in v7:
time: 40.5 us; the launch traced here: 40 us
  Pallas kernels  38.8 us (96%)
  local copies, waits for them, and re-layouts  1.15 us (3%)
    pallas_call x1, Pallas kernels, local(): pl.pallas_call(functools.partial(kernel, counts), out_shape=pltpu.VMEM((8...  38.8 us
    unnamed x1, local copies, waits for them, and re-layouts  1.15 us

profile of v7, /device:TPU:8, one launch (start us, length us, event | category | flops | bytes accessed | tf_op | source)
XLA Modules:
  0.0 40.0 jit_solution(154949633948186221)
XLA Ops:
  0.0 38.8 %shard_map.46 = f32[8,6,64,128]{3,2,1,0:T(8,128)S(1)} custom-call(f32[8,6,64,128]{3,2,1,0:T(8,128)} %bitcast.4, f32[3,4,16,128]{3,2,1,0:T(8,128)} %velocity_hbm.1, f32[4,16,128]{2,1,0:T(8,128)} %diffusivity_hbm.1, f32[3,8]{1,0:T(4,128)} %bitcast.5), custom_call_target="tpu_custom_call" | custom-call | tf_op jit(solution)/shard_map/pallas_call | solution.py:496
  38.8 1.1 %copy.6 = f32[8,6,4,16,128]{4,3,2,1,0:T(8,128)} copy(f32[8,6,4,16,128]{4,3,2,1,0:T(8,128)S(1)} %bitcast.3) | data formatting | bytes 3145728

commit v8 on v7

--- a/solution.py
+++ b/solution.py
@@ -76,6 +76,7 @@
     own_sem,
     relay_send,
     relay_recv,
+    x_sem,
     speed_send,
     speed_recv,
     send_sem,
@@ -151,11 +152,7 @@
         return face(k, two(c), way, recv_sem.at[k, c, way])
 
     def all_sent(way):
-        if way in to_relay:
-            all_x = p.at[:, :, 1, pl.ds(1, 16)]
-            copy_x((all_x, all_x), way, recv_sem.at[0, 0, way], target[way]).wait_send()
-        else:
-            face(pl.ds(0, 3), pl.ds(0, NS), way, recv_sem.at[0, 0, way]).wait_send()
+        face(pl.ds(0, 3), pl.ds(0, NS), way, recv_sem.at[0, 0, way]).wait_send()
 
     def x_face(k, c, way, s=None):
         src, dst = {EAST: (4, 0), WEST: (1, 5)}[way]
@@ -168,11 +165,11 @@
             refs = p.at[k, which, src, pl.ds(1, 16)], p.at[k, which, dst, pl.ds(1, 16)]
         return refs
 
-    def copy_x(refs, way, recv, to):
+    def copy_x(refs, way, k, c, recv, to):
         return pltpu.make_async_remote_copy(
             src_ref=refs[0],
             dst_ref=refs[1],
-            send_sem=send_sem.at[way],
+            send_sem=x_sem.at[way, (3 * k + c) % 2],
             recv_sem=recv,
             device_id=to,
             device_id_type=MESH,
@@ -181,21 +178,32 @@
     def relay_at(k, c):
         return raw_relay.at[c] if k == 0 else relay.at[k - 1, c]
 
+    def left_x(k, c):
+        for way in (EAST, WEST):
+
+            @pl.when(has[way])
+            def _():
+                copy_x(
+                    x_face(k, c, way), way, k, c, recv_sem.at[k, c, way], target[way]
+                ).wait_send()
+
     def send_x(k, c):
+        if 3 * k + c >= 2:
+            left_x(*divmod(3 * k + c - 2, 3))
         for way in (EAST, WEST):
             recv = recv_sem.at[k, c, way]
 
             @pl.when(has[way] & jnp.logical_not(to_relay[way]))
             def _():
-                copy_x(x_face(k, c, way), way, recv, target[way]).start()
+                copy_x(x_face(k, c, way), way, k, c, recv, target[way]).start()
 
             @pl.when(to_relay[way])
             def _():
                 src = x_face(k, c, way, 1)[0]
                 copy_x(
-                    (src, relay_at(k, c)), way, relay_recv.at[k, c], relay_of[way]
+                    (src, relay_at(k, c)), way, k, c, relay_recv.at[k, c], relay_of[way]
                 ).start()
-                copy_x(x_face(k, c, way, 0), way, recv, target[way]).start()
+                copy_x(x_face(k, c, way, 0), way, k, c, recv, target[way]).start()
 
     def send(k, c, way):
         pl.when(has[way])(lambda: chunk(k, c, way).start())
@@ -205,7 +213,9 @@
 
             @pl.when(has[back[way]])
             def _():
-                copy_x(x_face(k, c, way), way, recv_sem.at[k, c, way], target[way]).wait_recv()
+                copy_x(
+                    x_face(k, c, way), way, k, c, recv_sem.at[k, c, way], target[way]
+                ).wait_recv()
 
     def pass_on(k, c):
         for way in (EAST, WEST):
@@ -301,8 +311,7 @@
     send_x(0, 0)
     for way in (EAST, WEST, NORTH, SOUTH):
         pl.when(has[way])(lambda way=way: speed_face(way).start())
-    for c in range(1, PAIRS):
-        send_x(0, c)
+    send_x(0, 1)
 
     def second_exchange(k, c):
         chunk(k, c, SUM1).wait_recv()
@@ -396,6 +405,7 @@
         return 0
 
     lax.fori_loop(0, 4, coefficients, 0)
+    send_x(0, 2)
 
     def advance(k, c):
         base_weight, section_weight = WEIGHTS[k - 1]
@@ -468,10 +478,10 @@
                     pl.when(has[back[way]])(lambda way=way: turn_face(c, way))
             blocks(0, 3, 2, advance(k, c))
             if k < 3:
-                send_x(k, c)
                 for way in (NORTH, SOUTH):
                     send(k, c, way)
                 chunk(k, c, SUM1).start()
+                send_x(k, c)
             if c == 0:
                 pass_on(k - 1, PAIRS - 1)
                 second_exchange(k - 1, PAIRS - 1)
@@ -481,7 +491,10 @@
 
     for way in (EAST, WEST, NORTH, SOUTH):
         pl.when(has[way])(lambda way=way: speed_face(way).wait_send())
-        pl.when(has[way])(lambda way=way: all_sent(way))
+        if way not in to_relay:
+            pl.when(has[way])(lambda way=way: all_sent(way))
+    left_x(2, 1)
+    left_x(2, 2)
     all_passed_on()
     all_sent(SUM1)
     all_sent(SUM2)
@@ -521,6 +534,7 @@
             dma((5,)),
             dma,
             dma((3, PAIRS)),
+            dma((2, 2)),
             dma((4,)),
             dma((4,)),
             dma((6,)),

time: 40.5 us -> 41.6 us (1.027)
  the two profiles are of different devices: /device:TPU:8 before, /device:TPU:16 now
where the time goes in v8:
time: 41.6 us; the launch traced here: 41.5 us
  Pallas kernels  40.3 us (97%)
  local copies, waits for them, and re-layouts  1.15 us (3%)
    pallas_call x1, Pallas kernels, local(): pl.pallas_call(functools.partial(kernel, counts), out_shape=pltpu.VMEM((8...  40.3 us
    unnamed x1, local copies, waits for them, and re-layouts  1.15 us

profile of v8, /device:TPU:16, one launch (start us, length us, event | category | flops | bytes accessed | tf_op | source)
XLA Modules:
  0.0 41.5 jit_solution(4496224300783017867)
XLA Ops:
  0.0 40.3 %shard_map.46 = f32[8,6,64,128]{3,2,1,0:T(8,128)S(1)} custom-call(f32[8,6,64,128]{3,2,1,0:T(8,128)} %bitcast.4, f32[3,4,16,128]{3,2,1,0:T(8,128)} %velocity_hbm.1, f32[4,16,128]{2,1,0:T(8,128)} %diffusivity_hbm.1, f32[3,8]{1,0:T(4,128)} %bitcast.5), custom_call_target="tpu_custom_call" | custom-call | tf_op jit(solution)/shard_map/pallas_call | solution.py:509
  40.3 1.1 %copy.6 = f32[8,6,4,16,128]{4,3,2,1,0:T(8,128)} copy(f32[8,6,4,16,128]{4,3,2,1,0:T(8,128)S(1)} %bitcast.3) | data formatting | bytes 3145728

commit v9 on v7

--- a/solution.py
+++ b/solution.py
@@ -31,13 +31,13 @@
         + pltpu.roll(jnp.where(low, tiles[i + 4], tiles[i]), 4, 0)
         for i in range(4)
     ]
-    even = lax.rem(row, 4) < 2
+    even = (row & 2) == 0
     pairs = [
         jnp.where(even, quads[i], quads[i + 2])
         + jnp.where(even, pltpu.roll(quads[i], 6, 0), pltpu.roll(quads[i + 2], 2, 0))
         for i in range(2)
     ]
-    first = lax.rem(row, 2) < 1
+    first = (row & 1) == 0
     return jnp.where(first, pairs[0], pairs[1]) + jnp.where(
         first, pltpu.roll(pairs[0], 7, 0), pltpu.roll(pairs[1], 1, 0)
     )
@@ -234,12 +234,13 @@
     def arrived(k, c, way):
         pl.when(has[back[way]])(lambda: chunk(k, c, way).wait_recv())
 
-    def blocks(first, step, count, body):
+    def planes(first, step, count, body):
         def at(i, _):
-            body(first + step * (i // 2), lax.rem(i, 2))
+            for h in range(2):
+                body(first + step * i, h)
             return 0
 
-        lax.fori_loop(0, 2 * count, at, 0)
+        lax.fori_loop(0, count, at, 0)
 
     load_in(0).start()
     for copy in own:
@@ -274,21 +275,23 @@
     zero = jnp.zeros((8, 128), F32)
 
     def clear_x(x, speed):
-        def at(i, _):
-            for y in range(16):
-                p[i // NS, lax.rem(i, NS), x, 1 + y] = zero
+        def at(s, _):
+            for k in range(3):
+                for y in range(16):
+                    p[k, s, x, 1 + y] = zero
             return 0
 
-        lax.fori_loop(0, 3 * NS, at, 0)
+        lax.fori_loop(0, NS, at, 0)
         speed_x[speed] = jnp.zeros((16, 128), F32)
 
     def clear_y(y, speed):
-        def at(i, _):
-            for x in range(4):
-                p[i // NS, lax.rem(i, NS), 1 + x, y] = zero
+        def at(s, _):
+            for k in range(3):
+                for x in range(4):
+                    p[k, s, 1 + x, y] = zero
             return 0
 
-        lax.fori_loop(0, 3 * NS, at, 0)
+        lax.fori_loop(0, NS, at, 0)
         for x in range(4):
             speed_y[x, speed : speed + 8] = zero
 
@@ -330,20 +333,16 @@
     raw_rows = raw.reshape(2 * PAIRS * 8 * 32, 128)
 
     def turn_face(c, way):
-        def at(i, _):
-            j, h = i // 2, lax.rem(i, 2)
-            start = (way * PAIRS + c) * 256 + i * 8
-            tiles = [raw_rows[pl.ds(start + y, 8, stride=32), :] for y in range(8)]
-            for y in range(8):
-                p[0, 2 * c + j, 0 if way == EAST else 5, h * 8 + y + 1] = tiles[y]
-            return 0
-
-        lax.fori_loop(0, 4, at, 0)
+        for j in range(2):
+            start = (way * PAIRS + c) * 256 + j * 16
+            for y in range(16):
+                tile = raw_rows[pl.ds(start + y, 8, stride=32), :]
+                p[0, 2 * c + j, 0 if way == EAST else 5, y + 1] = tile
 
     for c in range(PAIRS):
         for s in (2 * c, 2 * c + 1):
             load_in(s).wait()
-            blocks(0, 1, 4, turn(s))
+            planes(0, 1, 4, turn(s))
         send(0, c, NORTH)
         send(0, c, SOUTH)
         chunk(0, c, SUM1).start()
@@ -461,12 +460,12 @@
             mean_term(k - 1, c)
             arrived(k - 1, c, NORTH)
             arrived(k - 1, c, SOUTH)
-            blocks(1, 1, 2, advance(k, c))
+            planes(1, 1, 2, advance(k, c))
             arrived_x(k - 1, c)
             if k == 1:
                 for way in (EAST, WEST):
                     pl.when(has[back[way]])(lambda way=way: turn_face(c, way))
-            blocks(0, 3, 2, advance(k, c))
+            planes(0, 3, 2, advance(k, c))
             if k < 3:
                 send_x(k, c)
                 for way in (NORTH, SOUTH):

time: 40.5 us -> 39.5 us (0.975)
  Pallas kernels: 38.8 us -> 38.1 us
    pallas_call x1, Pallas kernels: 38.8 us -> 38.1 us  [local(): pl.pallas_call(functools.partial(kernel, counts), out_shape=pltpu.VMEM((8...]
where the time goes in v9:
time: 39.5 us; the launch traced here: 39.3 us
  Pallas kernels  38.1 us (96%)
  local copies, waits for them, and re-layouts  1.15 us (3%)
    pallas_call x1, Pallas kernels, local(): pl.pallas_call(functools.partial(kernel, counts), out_shape=pltpu.VMEM((8...  38.1 us
    unnamed x1, local copies, waits for them, and re-layouts  1.15 us

profile of v9, /device:TPU:8, one launch (start us, length us, event | category | flops | bytes accessed | tf_op | source)
XLA Modules:
  0.0 39.3 jit_solution(9974008491700646485)
XLA Ops:
  0.0 38.1 %shard_map.46 = f32[8,6,64,128]{3,2,1,0:T(8,128)S(1)} custom-call(f32[8,6,64,128]{3,2,1,0:T(8,128)} %bitcast.4, f32[3,4,16,128]{3,2,1,0:T(8,128)} %velocity_hbm.1, f32[4,16,128]{2,1,0:T(8,128)} %diffusivity_hbm.1, f32[3,8]{1,0:T(4,128)} %bitcast.5), custom_call_target="tpu_custom_call" | custom-call | tf_op jit(solution)/shard_map/pallas_call | solution.py:495
  38.1 1.1 %copy.6 = f32[8,6,4,16,128]{4,3,2,1,0:T(8,128)} copy(f32[8,6,4,16,128]{4,3,2,1,0:T(8,128)S(1)} %bitcast.3) | data formatting | bytes 3145728

commit v10 on v9

--- a/solution.py
+++ b/solution.py
@@ -61,9 +61,8 @@
     weight,
     mean_row,
     part,
-    part_1,
-    half,
-    part_2,
+    part_in,
+    total,
     speed_x,
     speed_y,
     speed_z,
@@ -85,14 +84,11 @@
     ax, ix, iy = lax.axis_index("af"), lax.axis_index("gx"), lax.axis_index("gy")
     has = {EAST: ix < nx - 1, WEST: ix > 0, NORTH: iy < ny - 1, SOUTH: iy > 0}
     back = {EAST: WEST, WEST: EAST, NORTH: SOUTH, SOUTH: NORTH}
-    pair = {SUM1: ax + 1 - 2 * lax.rem(ax, 2), SUM2: na - 1 - ax}
     target = {
         EAST: {"gx": ix + 1},
         WEST: {"gx": ix - 1},
         NORTH: {"gy": iy + 1},
         SOUTH: {"gy": iy - 1},
-        SUM1: {"af": pair[SUM1]},
-        SUM2: {"af": pair[SUM2]},
     }
 
     mid, end = nx // 2, nx - 1
@@ -135,8 +131,6 @@
         src, dst = {
             NORTH: lambda: (p.at[k, s, pl.ds(1, 4), 16], p.at[k, s, pl.ds(1, 4), 0]),
             SOUTH: lambda: (p.at[k, s, pl.ds(1, 4), 1], p.at[k, s, pl.ds(1, 4), 17]),
-            SUM1: lambda: (part.at[k, s], part_1.at[k, s]),
-            SUM2: lambda: (half.at[k, s], part_2.at[k, s]),
         }[way]()
         return pltpu.make_async_remote_copy(
             src_ref=src,
@@ -249,7 +243,7 @@
         load_in(s).start()
 
     barrier = pltpu.get_barrier_semaphore()
-    expected = 2
+    expected = na - 1
     for way in (EAST, WEST, NORTH, SOUTH):
         pl.when(has[way])(
             lambda way=way: pl.semaphore_signal(
@@ -269,8 +263,9 @@
                 for partner in partners:
                     pl.semaphore_signal(barrier, inc=1, device_id=partner, device_id_type=MESH)
 
-    for way in (SUM1, SUM2):
-        pl.semaphore_signal(barrier, inc=1, device_id=target[way], device_id_type=MESH)
+    for step in range(1, na):
+        other = {"af": lax.rem(ax + step, na)}
+        pl.semaphore_signal(barrier, inc=1, device_id=other, device_id_type=MESH)
 
     zero = jnp.zeros((8, 128), F32)
 
@@ -307,16 +302,46 @@
     for c in range(1, PAIRS):
         send_x(0, c)
 
+    def scatter(k, c, owner):
+        @pl.when(ax != owner)
+        def _():
+            pltpu.make_async_remote_copy(
+                src_ref=part.at[k, two(c), owner],
+                dst_ref=part_in.at[k, c, lax.rem(owner - ax + na, na) - 1],
+                send_sem=send_sem.at[SUM1],
+                recv_sem=recv_sem.at[k, c, SUM1],
+                device_id={"af": owner},
+                device_id_type=MESH,
+            ).start()
+
+    def wait_bytes(ref, sem):
+        pltpu.make_async_copy(ref, ref, sem).wait()
+
     def second_exchange(k, c):
-        chunk(k, c, SUM1).wait_recv()
-        half[k, two(c)] = part[k, two(c)] + part_1[k, two(c)]
-        chunk(k, c, SUM2).start()
+        wait_bytes(part_in.at[k, c], recv_sem.at[k, c, SUM1])
+        for i in range(2):
+            total[k, 2 * c + i, ax] = (part[k, 2 * c + i, ax] + part_in[k, c, 0, i]) + (
+                part_in[k, c, 1, i] + part_in[k, c, 2, i]
+            )
+        for member in range(na):
+
+            @pl.when(ax != member)
+            def _():
+                mine = total.at[k, two(c), ax]
+                pltpu.make_async_remote_copy(
+                    src_ref=mine,
+                    dst_ref=mine,
+                    send_sem=send_sem.at[SUM2],
+                    recv_sem=recv_sem.at[k, c, SUM2],
+                    device_id={"af": member},
+                    device_id_type=MESH,
+                ).start()
 
     def mean_term(k, c):
-        chunk(k, c, SUM2).wait_recv()
+        wait_bytes(total.at[k, two(c), pl.ds(0, na - 1)], recv_sem.at[k, c, SUM2])
         scale = (STEP * MIX / FIELDS) * diffusion[...]
         for i in range(2):
-            mean_row[i] = scale * (half[k, 2 * c + i] + part_2[k, 2 * c + i])
+            mean_row[i] = scale * total[k, 2 * c + i]
 
     def turn(s):
         flat = rows_in.reshape(NS * 8 * 64, 128)
@@ -345,7 +370,8 @@
             planes(0, 1, 4, turn(s))
         send(0, c, NORTH)
         send(0, c, SOUTH)
-        chunk(0, c, SUM1).start()
+        for owner in range(na):
+            scatter(0, c, owner)
         if c > 0:
             pass_on(0, c - 1)
             second_exchange(0, c - 1)
@@ -461,6 +487,9 @@
             arrived(k - 1, c, NORTH)
             arrived(k - 1, c, SOUTH)
             planes(1, 1, 2, advance(k, c))
+            if k < 3:
+                scatter(k, c, 1)
+                scatter(k, c, 2)
             arrived_x(k - 1, c)
             if k == 1:
                 for way in (EAST, WEST):
@@ -468,9 +497,10 @@
             planes(0, 3, 2, advance(k, c))
             if k < 3:
                 send_x(k, c)
+                scatter(k, c, 0)
+                scatter(k, c, 3)
                 for way in (NORTH, SOUTH):
                     send(k, c, way)
-                chunk(k, c, SUM1).start()
             if c == 0:
                 pass_on(k - 1, PAIRS - 1)
                 second_exchange(k - 1, PAIRS - 1)
@@ -482,8 +512,8 @@
         pl.when(has[way])(lambda way=way: speed_face(way).wait_send())
         pl.when(has[way])(lambda way=way: all_sent(way))
     all_passed_on()
-    all_sent(SUM1)
-    all_sent(SUM2)
+    wait_bytes(part_in, send_sem.at[SUM1])
+    wait_bytes(part_in, send_sem.at[SUM2])
 
 
 def local(fields_state, velocity, diffusivity, wiener_draw):
@@ -505,8 +535,7 @@
             vmem(4, 16, 8, 128),
             vmem(2, 4, 16, 128),
             vmem(3, NS, 4, 16, 128),
-            vmem(3, NS, 4, 16, 128),
-            vmem(3, NS, 4, 16, 128),
+            vmem(3, PAIRS, 3, 2, 16, 128),
             vmem(3, NS, 4, 16, 128),
             vmem(6, 16, 128),
             vmem(4, 32, 128),

time: 39.5 us -> 39.3 us (level)
  no operation moved by 1% of the time
where the time goes in v10:
time: 39.3 us; the launch traced here: 39.2 us
  Pallas kernels  38 us (97%)
  local copies, waits for them, and re-layouts  1.15 us (3%)
    pallas_call x1, Pallas kernels, local(): pl.pallas_call(functools.partial(kernel, counts), out_shape=pltpu.VMEM((8...  38 us
    unnamed x1, local copies, waits for them, and re-layouts  1.15 us

profile of v10, /device:TPU:8, one launch (start us, length us, event | category | flops | bytes accessed | tf_op | source)
XLA Modules:
  0.0 39.2 jit_solution(2481843075799860812)
XLA Ops:
  0.0 38.0 %shard_map.46 = f32[8,6,64,128]{3,2,1,0:T(8,128)S(1)} custom-call(f32[8,6,64,128]{3,2,1,0:T(8,128)} %bitcast.4, f32[3,4,16,128]{3,2,1,0:T(8,128)} %velocity_hbm.1, f32[4,16,128]{2,1,0:T(8,128)} %diffusivity_hbm.1, f32[3,8]{1,0:T(4,128)} %bitcast.5), custom_call_target="tpu_custom_call" | custom-call | tf_op jit(solution)/shard_map/pallas_call | solution.py:525
  38.0 1.1 %copy.6 = f32[8,6,4,16,128]{4,3,2,1,0:T(8,128)} copy(f32[8,6,4,16,128]{4,3,2,1,0:T(8,128)S(1)} %bitcast.3) | data formatting | bytes 3145728

commit v11 on v10

--- a/solution.py
+++ b/solution.py
@@ -85,17 +85,22 @@
     has = {EAST: ix < nx - 1, WEST: ix > 0, NORTH: iy < ny - 1, SOUTH: iy > 0}
     back = {EAST: WEST, WEST: EAST, NORTH: SOUTH, SOUTH: NORTH}
     target = {
-        EAST: {"gx": ix + 1},
-        WEST: {"gx": ix - 1},
-        NORTH: {"gy": iy + 1},
-        SOUTH: {"gy": iy - 1},
+        EAST: (ax, ix + 1, iy),
+        WEST: (ax, ix - 1, iy),
+        NORTH: (ax, ix, iy + 1),
+        SOUTH: (ax, ix, iy - 1),
     }
+    members = [lax.rem(ax + step, na) for step in range(na)]
+    member_ids = [(other, ix, iy) for other in members]
 
     mid, end = nx // 2, nx - 1
     to_relay = {EAST: ix == mid - 1, WEST: ix == mid}
     is_relay = {EAST: ix == end, WEST: ix == 0}
-    relay_of = {EAST: {"gx": end}, WEST: {"gx": 0}}
-    relay_to = {EAST: {"gx": mid}, WEST: {"gx": mid - 1}}
+    relay_of = {EAST: (ax, end, iy), WEST: (ax, 0, iy)}
+    relay_to = {EAST: (ax, mid, iy), WEST: (ax, mid - 1, iy)}
+    is_mid, is_end = to_relay[EAST] | to_relay[WEST], is_relay[EAST] | is_relay[WEST]
+    both = {EAST: has[EAST] & has[WEST], NORTH: has[NORTH] & has[SOUTH]}
+    plain = {way: has[way] & jnp.logical_not(to_relay[way]) for way in (EAST, WEST)}
 
     def load_in(s):
         return pltpu.make_async_copy(fields_hbm.at[:, s], rows_in.at[s], in_sem.at[s])
@@ -142,14 +147,16 @@
         )
 
     def chunk(k, c, way):
-        return face(k, two(c), way, recv_sem.at[k, c, way])
+        return face(k, two(c), way, recv_sem.at[k, c, NORTH])
+
+    def wait_bytes(ref, sem):
+        pltpu.make_async_copy(ref, ref, sem).wait()
 
     def all_sent(way):
         if way in to_relay:
-            all_x = p.at[:, :, 1, pl.ds(1, 16)]
-            copy_x((all_x, all_x), way, recv_sem.at[0, 0, way], target[way]).wait_send()
+            wait_bytes(p.at[:, :, 1, pl.ds(1, 16)], send_sem.at[way])
         else:
-            face(pl.ds(0, 3), pl.ds(0, NS), way, recv_sem.at[0, 0, way]).wait_send()
+            wait_bytes(p.at[:, :, pl.ds(1, 4), 1], send_sem.at[way])
 
     def x_face(k, c, way, s=None):
         src, dst = {EAST: (4, 0), WEST: (1, 5)}[way]
@@ -176,57 +183,69 @@
         return raw_relay.at[c] if k == 0 else relay.at[k - 1, c]
 
     def send_x(k, c):
+        recv = recv_sem.at[k, c, EAST]
         for way in (EAST, WEST):
-            recv = recv_sem.at[k, c, way]
-
-            @pl.when(has[way] & jnp.logical_not(to_relay[way]))
+
+            @pl.when(plain[way])
             def _():
                 copy_x(x_face(k, c, way), way, recv, target[way]).start()
 
-            @pl.when(to_relay[way])
-            def _():
-                src = x_face(k, c, way, 1)[0]
-                copy_x(
-                    (src, relay_at(k, c)), way, relay_recv.at[k, c], relay_of[way]
-                ).start()
-                copy_x(x_face(k, c, way, 0), way, recv, target[way]).start()
-
-    def send(k, c, way):
-        pl.when(has[way])(lambda: chunk(k, c, way).start())
+        @pl.when(is_mid)
+        def _():
+            for way in (EAST, WEST):
+
+                @pl.when(to_relay[way])
+                def _():
+                    src = x_face(k, c, way, 1)[0]
+                    copy_x(
+                        (src, relay_at(k, c)), way, relay_recv.at[k, c], relay_of[way]
+                    ).start()
+                    copy_x(x_face(k, c, way, 0), way, recv, target[way]).start()
+
+    def send_y(k, c):
+        for way in (NORTH, SOUTH):
+            pl.when(has[way])(lambda: chunk(k, c, way).start())
+
+    def arrived_y(k, c):
+        sem = recv_sem.at[k, c, NORTH]
+        two_faces = p.at[k, two(c), pl.ds(1, 4), pl.ds(0, 2)]
+        one_face = p.at[k, two(c), pl.ds(1, 4), pl.ds(0, 1)]
+        pl.when(both[NORTH])(lambda: wait_bytes(two_faces, sem))
+        pl.when(jnp.logical_not(both[NORTH]))(lambda: wait_bytes(one_face, sem))
 
     def arrived_x(k, c):
-        for way in (EAST, WEST):
-
-            @pl.when(has[back[way]])
-            def _():
-                copy_x(x_face(k, c, way), way, recv_sem.at[k, c, way], target[way]).wait_recv()
+        sem = recv_sem.at[k, c, EAST]
+        if k == 0:
+            two_faces, one_face = raw.at[:, c], raw.at[0, c]
+        else:
+            two_faces = p.at[k, two(c), pl.ds(0, 2), pl.ds(1, 16)]
+            one_face = p.at[k, two(c), pl.ds(0, 1), pl.ds(1, 16)]
+        pl.when(both[EAST])(lambda: wait_bytes(two_faces, sem))
+        pl.when(jnp.logical_not(both[EAST]))(lambda: wait_bytes(one_face, sem))
 
     def pass_on(k, c):
-        for way in (EAST, WEST):
-
-            @pl.when(is_relay[way])
-            def _():
-                here = relay_at(k, c)
-                pltpu.make_async_copy(here, here, relay_recv.at[k, c]).wait()
-                pltpu.make_async_remote_copy(
-                    src_ref=here,
-                    dst_ref=x_face(k, c, way, 1)[1],
-                    send_sem=relay_send,
-                    recv_sem=recv_sem.at[k, c, way],
-                    device_id=relay_to[way],
-                    device_id_type=MESH,
-                ).start()
+        @pl.when(is_end)
+        def _():
+            here = relay_at(k, c)
+            wait_bytes(here, relay_recv.at[k, c])
+            for way in (EAST, WEST):
+
+                @pl.when(is_relay[way])
+                def _():
+                    pltpu.make_async_remote_copy(
+                        src_ref=here,
+                        dst_ref=x_face(k, c, way, 1)[1],
+                        send_sem=relay_send,
+                        recv_sem=recv_sem.at[k, c, EAST],
+                        device_id=relay_to[way],
+                        device_id_type=MESH,
+                    ).start()
 
     def all_passed_on():
-        for way in (EAST, WEST):
-
-            @pl.when(is_relay[way])
-            def _():
-                pltpu.make_async_copy(relay, relay, relay_send).wait()
-                pltpu.make_async_copy(raw_relay, raw_relay, relay_send).wait()
-
-    def arrived(k, c, way):
-        pl.when(has[back[way]])(lambda: chunk(k, c, way).wait_recv())
+        @pl.when(is_end)
+        def _():
+            wait_bytes(relay, relay_send)
+            wait_bytes(raw_relay, relay_send)
 
     def planes(first, step, count, body):
         def at(i, _):
@@ -253,8 +272,8 @@
         expected = expected + has[way].astype(jnp.int32)
     for way in (EAST, WEST):
         for near, partners in (
-            (to_relay[way], ({"gx": 0}, {"gx": end})),
-            (is_relay[way], ({"gx": mid - 1}, {"gx": mid})),
+            (to_relay[way], ((ax, 0, iy), (ax, end, iy))),
+            (is_relay[way], ((ax, mid - 1, iy), (ax, mid, iy))),
         ):
             expected = expected + 2 * near.astype(jnp.int32)
 
@@ -264,8 +283,9 @@
                     pl.semaphore_signal(barrier, inc=1, device_id=partner, device_id_type=MESH)
 
     for step in range(1, na):
-        other = {"af": lax.rem(ax + step, na)}
-        pl.semaphore_signal(barrier, inc=1, device_id=other, device_id_type=MESH)
+        pl.semaphore_signal(
+            barrier, inc=1, device_id=member_ids[step], device_id_type=MESH
+        )
 
     zero = jnp.zeros((8, 128), F32)
 
@@ -302,20 +322,16 @@
     for c in range(1, PAIRS):
         send_x(0, c)
 
-    def scatter(k, c, owner):
-        @pl.when(ax != owner)
-        def _():
+    def scatter(k, c):
+        for step in range(1, na):
             pltpu.make_async_remote_copy(
-                src_ref=part.at[k, two(c), owner],
-                dst_ref=part_in.at[k, c, lax.rem(owner - ax + na, na) - 1],
+                src_ref=part.at[k, two(c), members[step]],
+                dst_ref=part_in.at[k, c, step - 1],
                 send_sem=send_sem.at[SUM1],
                 recv_sem=recv_sem.at[k, c, SUM1],
-                device_id={"af": owner},
+                device_id=member_ids[step],
                 device_id_type=MESH,
             ).start()
-
-    def wait_bytes(ref, sem):
-        pltpu.make_async_copy(ref, ref, sem).wait()
 
     def second_exchange(k, c):
         wait_bytes(part_in.at[k, c], recv_sem.at[k, c, SUM1])
@@ -323,19 +339,16 @@
             total[k, 2 * c + i, ax] = (part[k, 2 * c + i, ax] + part_in[k, c, 0, i]) + (
                 part_in[k, c, 1, i] + part_in[k, c, 2, i]
             )
-        for member in range(na):
-
-            @pl.when(ax != member)
-            def _():
-                mine = total.at[k, two(c), ax]
-                pltpu.make_async_remote_copy(
-                    src_ref=mine,
-                    dst_ref=mine,
-                    send_sem=send_sem.at[SUM2],
-                    recv_sem=recv_sem.at[k, c, SUM2],
-                    device_id={"af": member},
-                    device_id_type=MESH,
-                ).start()
+        mine = total.at[k, two(c), ax]
+        for step in range(1, na):
+            pltpu.make_async_remote_copy(
+                src_ref=mine,
+                dst_ref=mine,
+                send_sem=send_sem.at[SUM2],
+                recv_sem=recv_sem.at[k, c, SUM2],
+                device_id=member_ids[step],
+                device_id_type=MESH,
+            ).start()
 
     def mean_term(k, c):
         wait_bytes(total.at[k, two(c), pl.ds(0, na - 1)], recv_sem.at[k, c, SUM2])
@@ -368,10 +381,8 @@
         for s in (2 * c, 2 * c + 1):
             load_in(s).wait()
             planes(0, 1, 4, turn(s))
-        send(0, c, NORTH)
-        send(0, c, SOUTH)
-        for owner in range(na):
-            scatter(0, c, owner)
+        scatter(0, c)
+        send_y(0, c)
         if c > 0:
             pass_on(0, c - 1)
             second_exchange(0, c - 1)
@@ -387,8 +398,8 @@
     draws = []
     for d in range(3):
         row = jnp.broadcast_to(wiener[d : d + 1, :], (8, 8))
-        column = jnp.sum(jnp.where(diagonal, row, 0.0), axis=1, keepdims=True)
-        draws.append(jnp.broadcast_to(column, (8, 128)))
+        draw = jnp.sum(jnp.where(diagonal, row, 0.0), axis=1, keepdims=True)
+        draws.append(jnp.broadcast_to(draw, (8, 128)))
 
     def coefficients(x, _):
         g = diffusion[x]
@@ -484,12 +495,8 @@
     for k in range(1, 4):
         for c in range(PAIRS):
             mean_term(k - 1, c)
-            arrived(k - 1, c, NORTH)
-            arrived(k - 1, c, SOUTH)
+            arrived_y(k - 1, c)
             planes(1, 1, 2, advance(k, c))
-            if k < 3:
-                scatter(k, c, 1)
-                scatter(k, c, 2)
             arrived_x(k - 1, c)
             if k == 1:
                 for way in (EAST, WEST):
@@ -497,10 +504,8 @@
             planes(0, 3, 2, advance(k, c))
             if k < 3:
                 send_x(k, c)
-                scatter(k, c, 0)
-                scatter(k, c, 3)
-                for way in (NORTH, SOUTH):
-                    send(k, c, way)
+                scatter(k, c)
+                send_y(k, c)
             if c == 0:
                 pass_on(k - 1, PAIRS - 1)
                 second_exchange(k - 1, PAIRS - 1)

time: 39.3 us -> 40.4 us (1.028)
  Pallas kernels: 38 us -> 39.1 us
    pallas_call x1, Pallas kernels: 38 us -> 39.1 us  [local(): pl.pallas_call(functools.partial(kernel, counts), out_shape=pltpu.VMEM((8...]
where the time goes in v11:
time: 40.4 us; the launch traced here: 40.3 us
  Pallas kernels  39.1 us (97%)
  local copies, waits for them, and re-layouts  1.15 us (3%)
    pallas_call x1, Pallas kernels, local(): pl.pallas_call(functools.partial(kernel, counts), out_shape=pltpu.VMEM((8...  39.1 us
    unnamed x1, local copies, waits for them, and re-layouts  1.15 us

profile of v11, /device:TPU:8, one launch (start us, length us, event | category | flops | bytes accessed | tf_op | source)
XLA Modules:
  0.0 40.3 jit_solution(8795516265691107848)
XLA Ops:
  0.0 39.1 %shard_map.46 = f32[8,6,64,128]{3,2,1,0:T(8,128)S(1)} custom-call(f32[8,6,64,128]{3,2,1,0:T(8,128)} %bitcast.4, f32[3,4,16,128]{3,2,1,0:T(8,128)} %velocity_hbm.1, f32[4,16,128]{2,1,0:T(8,128)} %diffusivity_hbm.1, f32[3,8]{1,0:T(4,128)} %bitcast.5), custom_call_target="tpu_custom_call" | custom-call | tf_op jit(solution)/shard_map/pallas_call | solution.py:530
  39.1 1.1 %copy.6 = f32[8,6,4,16,128]{4,3,2,1,0:T(8,128)} copy(f32[8,6,4,16,128]{4,3,2,1,0:T(8,128)S(1)} %bitcast.3) | data formatting | bytes 3145728

commit v12 on v11

--- a/solution.py
+++ b/solution.py
@@ -319,17 +319,16 @@
     send_x(0, 0)
     for way in (EAST, WEST, NORTH, SOUTH):
         pl.when(has[way])(lambda way=way: speed_face(way).start())
-    for c in range(1, PAIRS):
-        send_x(0, c)
-
-    def scatter(k, c):
-        for step in range(1, na):
+
+    def scatter(k, c, owner):
+        @pl.when(ax != owner)
+        def _():
             pltpu.make_async_remote_copy(
-                src_ref=part.at[k, two(c), members[step]],
-                dst_ref=part_in.at[k, c, step - 1],
+                src_ref=part.at[k, two(c), owner],
+                dst_ref=part_in.at[k, c, lax.rem(owner - ax + na, na) - 1],
                 send_sem=send_sem.at[SUM1],
                 recv_sem=recv_sem.at[k, c, SUM1],
-                device_id=member_ids[step],
+                device_id=(owner, ix, iy),
                 device_id_type=MESH,
             ).start()
 
@@ -376,30 +375,6 @@
             for y in range(16):
                 tile = raw_rows[pl.ds(start + y, 8, stride=32), :]
                 p[0, 2 * c + j, 0 if way == EAST else 5, y + 1] = tile
-
-    for c in range(PAIRS):
-        for s in (2 * c, 2 * c + 1):
-            load_in(s).wait()
-            planes(0, 1, 4, turn(s))
-        scatter(0, c)
-        send_y(0, c)
-        if c > 0:
-            pass_on(0, c - 1)
-            second_exchange(0, c - 1)
-
-    for copy in own:
-        copy.wait()
-    for way in (EAST, WEST, NORTH, SOUTH):
-        pl.when(has[back[way]])(lambda way=way: speed_face(way).wait_recv())
-
-    diagonal = lax.broadcasted_iota(jnp.int32, (8, 8), 0) == lax.broadcasted_iota(
-        jnp.int32, (8, 8), 1
-    )
-    draws = []
-    for d in range(3):
-        row = jnp.broadcast_to(wiener[d : d + 1, :], (8, 8))
-        draw = jnp.sum(jnp.where(diagonal, row, 0.0), axis=1, keepdims=True)
-        draws.append(jnp.broadcast_to(draw, (8, 128)))
 
     def coefficients(x, _):
         g = diffusion[x]
@@ -431,7 +406,38 @@
             centre[1, x, y] = keep_y - STEP * OXIDATION
         return 0
 
+    def turn_pair(c):
+        for s in (2 * c, 2 * c + 1):
+            load_in(s).wait()
+            planes(0, 1, 4, turn(s))
+        if c + 1 < PAIRS:
+            send_x(0, c + 1)
+        for owner in range(na):
+            scatter(0, c, owner)
+        send_y(0, c)
+
+    turn_pair(0)
+    for copy in own:
+        copy.wait()
+    for way in (EAST, WEST, NORTH, SOUTH):
+        pl.when(has[back[way]])(lambda way=way: speed_face(way).wait_recv())
+
+    diagonal = lax.broadcasted_iota(jnp.int32, (8, 8), 0) == lax.broadcasted_iota(
+        jnp.int32, (8, 8), 1
+    )
+    draws = []
+    for d in range(3):
+        row = jnp.broadcast_to(wiener[d : d + 1, :], (8, 8))
+        draw = jnp.sum(jnp.where(diagonal, row, 0.0), axis=1, keepdims=True)
+        draws.append(jnp.broadcast_to(draw, (8, 128)))
+
     lax.fori_loop(0, 4, coefficients, 0)
+    turn_pair(1)
+    pass_on(0, 0)
+    second_exchange(0, 0)
+    turn_pair(2)
+    pass_on(0, 1)
+    second_exchange(0, 1)
 
     def advance(k, c):
         base_weight, section_weight = WEIGHTS[k - 1]
@@ -497,20 +503,26 @@
             mean_term(k - 1, c)
             arrived_y(k - 1, c)
             planes(1, 1, 2, advance(k, c))
+            if k < 3:
+                scatter(k, c, 1)
+                scatter(k, c, 2)
             arrived_x(k - 1, c)
+            if c == 0:
+                pass_on(k - 1, PAIRS - 1)
+            elif k < 3:
+                pass_on(k, c - 1)
             if k == 1:
                 for way in (EAST, WEST):
                     pl.when(has[back[way]])(lambda way=way: turn_face(c, way))
             planes(0, 3, 2, advance(k, c))
             if k < 3:
                 send_x(k, c)
-                scatter(k, c)
+                scatter(k, c, 0)
+                scatter(k, c, 3)
                 send_y(k, c)
             if c == 0:
-                pass_on(k - 1, PAIRS - 1)
                 second_exchange(k - 1, PAIRS - 1)
             elif k < 3:
-                pass_on(k, c - 1)
                 second_exchange(k, c - 1)
 
     for way in (EAST, WEST, NORTH, SOUTH):

time: 40.4 us -> 44.4 us (1.099)
  the two profiles are of different devices: /device:TPU:8 before, /device:TPU:2 now
where the time goes in v12:
time: 44.4 us
  Pallas kernels  43.2 us (97%)
  local copies, waits for them, and re-layouts  1.15 us (3%)
    pallas_call x1, Pallas kernels, local(): pl.pallas_call(functools.partial(kernel, counts), out_shape=pltpu.VMEM((8...  43.2 us
    unnamed x1, local copies, waits for them, and re-layouts  1.15 us

profile of v12, /device:TPU:2, one launch (start us, length us, event | category | flops | bytes accessed | tf_op | source)
XLA Modules:
  0.0 44.4 jit_solution(3737779629933619683)
XLA Ops:
  0.0 43.2 %shard_map.46 = f32[8,6,64,128]{3,2,1,0:T(8,128)S(1)} custom-call(f32[8,6,64,128]{3,2,1,0:T(8,128)} %bitcast.4, f32[3,4,16,128]{3,2,1,0:T(8,128)} %velocity_hbm.1, f32[4,16,128]{2,1,0:T(8,128)} %diffusivity_hbm.1, f32[3,8]{1,0:T(4,128)} %bitcast.5), custom_call_target="tpu_custom_call" | custom-call | tf_op jit(solution)/shard_map/pallas_call | solution.py:542
  43.2 1.1 %copy.6 = f32[8,6,4,16,128]{4,3,2,1,0:T(8,128)} copy(f32[8,6,4,16,128]{4,3,2,1,0:T(8,128)S(1)} %bitcast.3) | data formatting | bytes 3145728

commit v13 on v11

--- a/solution.py
+++ b/solution.py
@@ -319,17 +319,16 @@
     send_x(0, 0)
     for way in (EAST, WEST, NORTH, SOUTH):
         pl.when(has[way])(lambda way=way: speed_face(way).start())
-    for c in range(1, PAIRS):
-        send_x(0, c)
-
-    def scatter(k, c):
-        for step in range(1, na):
+
+    def scatter(k, c, owner):
+        @pl.when(ax != owner)
+        def _():
             pltpu.make_async_remote_copy(
-                src_ref=part.at[k, two(c), members[step]],
-                dst_ref=part_in.at[k, c, step - 1],
+                src_ref=part.at[k, two(c), owner],
+                dst_ref=part_in.at[k, c, lax.rem(owner - ax + na, na) - 1],
                 send_sem=send_sem.at[SUM1],
                 recv_sem=recv_sem.at[k, c, SUM1],
-                device_id=member_ids[step],
+                device_id=(owner, ix, iy),
                 device_id_type=MESH,
             ).start()
 
@@ -381,11 +380,14 @@
         for s in (2 * c, 2 * c + 1):
             load_in(s).wait()
             planes(0, 1, 4, turn(s))
-        scatter(0, c)
+        for owner in range(na):
+            scatter(0, c, owner)
         send_y(0, c)
         if c > 0:
+            second_exchange(0, c - 1)
             pass_on(0, c - 1)
-            second_exchange(0, c - 1)
+        if c + 1 < PAIRS:
+            send_x(0, c + 1)
 
     for copy in own:
         copy.wait()
@@ -497,21 +499,26 @@
             mean_term(k - 1, c)
             arrived_y(k - 1, c)
             planes(1, 1, 2, advance(k, c))
+            if k < 3:
+                scatter(k, c, 1)
+                scatter(k, c, 2)
             arrived_x(k - 1, c)
             if k == 1:
                 for way in (EAST, WEST):
                     pl.when(has[back[way]])(lambda way=way: turn_face(c, way))
             planes(0, 3, 2, advance(k, c))
             if k < 3:
-                send_x(k, c)
-                scatter(k, c)
+                scatter(k, c, 0)
+                scatter(k, c, 3)
                 send_y(k, c)
             if c == 0:
+                second_exchange(k - 1, PAIRS - 1)
                 pass_on(k - 1, PAIRS - 1)
-                second_exchange(k - 1, PAIRS - 1)
             elif k < 3:
+                second_exchange(k, c - 1)
                 pass_on(k, c - 1)
-                second_exchange(k, c - 1)
+            if k < 3:
+                send_x(k, c)
 
     for way in (EAST, WEST, NORTH, SOUTH):
         pl.when(has[way])(lambda way=way: speed_face(way).wait_send())

time: 40.4 us -> 41.3 us (1.022)
  Pallas kernels: 39.1 us -> 40.1 us
    pallas_call x1, Pallas kernels: 39.1 us -> 40.1 us  [local(): pl.pallas_call(functools.partial(kernel, counts), out_shape=pltpu.VMEM((8...]
where the time goes in v13:
time: 41.3 us; the launch traced here: 41.2 us
  Pallas kernels  40.1 us (97%)
  local copies, waits for them, and re-layouts  1.15 us (3%)
    pallas_call x1, Pallas kernels, local(): pl.pallas_call(functools.partial(kernel, counts), out_shape=pltpu.VMEM((8...  40.1 us
    unnamed x1, local copies, waits for them, and re-layouts  1.15 us

profile of v13, /device:TPU:8, one launch (start us, length us, event | category | flops | bytes accessed | tf_op | source)
XLA Modules:
  0.0 41.2 jit_solution(14727807442983928694)
XLA Ops:
  0.0 40.1 %shard_map.46 = f32[8,6,64,128]{3,2,1,0:T(8,128)S(1)} custom-call(f32[8,6,64,128]{3,2,1,0:T(8,128)} %bitcast.4, f32[3,4,16,128]{3,2,1,0:T(8,128)} %velocity_hbm.1, f32[4,16,128]{2,1,0:T(8,128)} %diffusivity_hbm.1, f32[3,8]{1,0:T(4,128)} %bitcast.5), custom_call_target="tpu_custom_call" | custom-call | tf_op jit(solution)/shard_map/pallas_call | solution.py:537
  40.1 1.1 %copy.6 = f32[8,6,4,16,128]{4,3,2,1,0:T(8,128)} copy(f32[8,6,4,16,128]{4,3,2,1,0:T(8,128)S(1)} %bitcast.3) | data formatting | bytes 3145728

commit v14 on v13

--- a/solution.py
+++ b/solution.py
@@ -99,6 +99,7 @@
     relay_of = {EAST: (ax, end, iy), WEST: (ax, 0, iy)}
     relay_to = {EAST: (ax, mid, iy), WEST: (ax, mid - 1, iy)}
     is_mid, is_end = to_relay[EAST] | to_relay[WEST], is_relay[EAST] | is_relay[WEST]
+    yields = lax.rem(iy, 2) == 1
     both = {EAST: has[EAST] & has[WEST], NORTH: has[NORTH] & has[SOUTH]}
     plain = {way: has[way] & jnp.logical_not(to_relay[way]) for way in (EAST, WEST)}
 
@@ -154,20 +155,21 @@
 
     def all_sent(way):
         if way in to_relay:
-            wait_bytes(p.at[:, :, 1, pl.ds(1, 16)], send_sem.at[way])
+            pl.when(jnp.logical_not(yields))(
+                lambda: wait_bytes(p.at[:, :, 1, pl.ds(1, 16)], send_sem.at[way])
+            )
         else:
             wait_bytes(p.at[:, :, pl.ds(1, 4), 1], send_sem.at[way])
 
-    def x_face(k, c, way, s=None):
+    def x_face(k, c, way, s=None, y=0, count=16):
         src, dst = {EAST: (4, 0), WEST: (1, 5)}[way]
-        side = way
         which = pl.ds(2 * c, 2) if s is None else pl.ds(2 * c + s, 1)
         to = pl.ds(0, 2) if s is None else pl.ds(s, 1)
         if k == 0:
-            refs = fields_hbm.at[:, which, pl.ds(16 * (src - 1), 16)], raw.at[side, c, :, to]
-        else:
-            refs = p.at[k, which, src, pl.ds(1, 16)], p.at[k, which, dst, pl.ds(1, 16)]
-        return refs
+            rows = pl.ds(16 * (src - 1) + y, count)
+            return fields_hbm.at[:, which, rows], raw.at[way, c, :, to, pl.ds(y, count)]
+        rows = pl.ds(1 + y, count)
+        return p.at[k, which, src, rows], p.at[k, which, dst, rows]
 
     def copy_x(refs, way, recv, to):
         return pltpu.make_async_remote_copy(
@@ -182,7 +184,15 @@
     def relay_at(k, c):
         return raw_relay.at[c] if k == 0 else relay.at[k - 1, c]
 
+    def left_x():
+        for way in (EAST, WEST):
+            pl.when(has[way] & yields)(
+                lambda: wait_bytes(p.at[1, two(0), 1, pl.ds(1, 16)], send_sem.at[way])
+            )
+
     def send_x(k, c):
+        if k or c:
+            left_x()
         recv = recv_sem.at[k, c, EAST]
         for way in (EAST, WEST):
 
@@ -196,11 +206,12 @@
 
                 @pl.when(to_relay[way])
                 def _():
-                    src = x_face(k, c, way, 1)[0]
+                    src = x_face(k, c, way, 1, 8, 8)[0]
                     copy_x(
                         (src, relay_at(k, c)), way, relay_recv.at[k, c], relay_of[way]
                     ).start()
                     copy_x(x_face(k, c, way, 0), way, recv, target[way]).start()
+                    copy_x(x_face(k, c, way, 1, 0, 8), way, recv, target[way]).start()
 
     def send_y(k, c):
         for way in (NORTH, SOUTH):
@@ -234,7 +245,7 @@
                 def _():
                     pltpu.make_async_remote_copy(
                         src_ref=here,
-                        dst_ref=x_face(k, c, way, 1)[1],
+                        dst_ref=x_face(k, c, way, 1, 8, 8)[1],
                         send_sem=relay_send,
                         recv_sem=recv_sem.at[k, c, EAST],
                         device_id=relay_to[way],
@@ -503,6 +514,10 @@
                 scatter(k, c, 1)
                 scatter(k, c, 2)
             arrived_x(k - 1, c)
+            if c == 0:
+                pass_on(k - 1, PAIRS - 1)
+            elif k < 3:
+                pass_on(k, c - 1)
             if k == 1:
                 for way in (EAST, WEST):
                     pl.when(has[back[way]])(lambda way=way: turn_face(c, way))
@@ -513,16 +528,15 @@
                 send_y(k, c)
             if c == 0:
                 second_exchange(k - 1, PAIRS - 1)
-                pass_on(k - 1, PAIRS - 1)
             elif k < 3:
                 second_exchange(k, c - 1)
-                pass_on(k, c - 1)
             if k < 3:
                 send_x(k, c)
 
     for way in (EAST, WEST, NORTH, SOUTH):
         pl.when(has[way])(lambda way=way: speed_face(way).wait_send())
         pl.when(has[way])(lambda way=way: all_sent(way))
+    left_x()
     all_passed_on()
     wait_bytes(part_in, send_sem.at[SUM1])
     wait_bytes(part_in, send_sem.at[SUM2])
@@ -554,9 +568,9 @@
             vmem(4, 16, 128),
             vmem(4, 16, 128),
             vmem(3, 8),
-            vmem(2, PAIRS, 1, 16, 8, 128),
+            vmem(2, PAIRS, 1, 8, 8, 128),
             vmem(2, PAIRS, 8, 2, 16, 128),
-            vmem(PAIRS, 8, 1, 16, 128),
+            vmem(PAIRS, 8, 1, 8, 128),
             dma((NS,)),
             dma((5,)),
             dma,

time: 41.3 us -> 42 us (1.017)
  the two profiles are of different devices: /device:TPU:8 before, /device:TPU:1 now
where the time goes in v14:
time: 42 us; the launch traced here: 41.9 us
  Pallas kernels  40.7 us (97%)
  local copies, waits for them, and re-layouts  1.15 us (3%)
    pallas_call x1, Pallas kernels, local(): pl.pallas_call(functools.partial(kernel, counts), out_shape=pltpu.VMEM((8...  40.7 us
    unnamed x1, local copies, waits for them, and re-layouts  1.15 us

profile of v14, /device:TPU:1, one launch (start us, length us, event | category | flops | bytes accessed | tf_op | source)
XLA Modules:
  0.0 41.9 jit_solution(10715673660353360928)
XLA Ops:
  0.0 40.7 %shard_map.46 = f32[8,6,64,128]{3,2,1,0:T(8,128)S(1)} custom-call(f32[8,6,64,128]{3,2,1,0:T(8,128)} %bitcast.4, f32[3,4,16,128]{3,2,1,0:T(8,128)} %velocity_hbm.1, f32[4,16,128]{2,1,0:T(8,128)} %diffusivity_hbm.1, f32[3,8]{1,0:T(4,128)} %bitcast.5), custom_call_target="tpu_custom_call" | custom-call | tf_op jit(solution)/shard_map/pallas_call | solution.py:551
  40.7 1.1 %copy.6 = f32[8,6,4,16,128]{4,3,2,1,0:T(8,128)} copy(f32[8,6,4,16,128]{4,3,2,1,0:T(8,128)S(1)} %bitcast.3) | data formatting | bytes 3145728

commit v15 on v13

--- a/solution.py
+++ b/solution.py
@@ -23,24 +23,10 @@
 EAST, WEST, NORTH, SOUTH, SUM1, SUM2 = range(6)
 
 
-def sum_rows(tiles):
-    row = lax.broadcasted_iota(jnp.int32, (8, 128), 0)
-    low = row < 4
-    quads = [
-        jnp.where(low, tiles[i], tiles[i + 4])
-        + pltpu.roll(jnp.where(low, tiles[i + 4], tiles[i]), 4, 0)
-        for i in range(4)
-    ]
-    even = (row & 2) == 0
-    pairs = [
-        jnp.where(even, quads[i], quads[i + 2])
-        + jnp.where(even, pltpu.roll(quads[i], 6, 0), pltpu.roll(quads[i + 2], 2, 0))
-        for i in range(2)
-    ]
-    first = (row & 1) == 0
-    return jnp.where(first, pairs[0], pairs[1]) + jnp.where(
-        first, pltpu.roll(pairs[0], 7, 0), pltpu.roll(pairs[1], 1, 0)
-    )
+def add_up(tiles):
+    while len(tiles) > 1:
+        tiles = [a + b for a, b in zip(tiles[::2], tiles[1::2])]
+    return tiles[0]
 
 
 def spread(rows, i):
@@ -363,7 +349,9 @@
             tiles = [flat[pl.ds(start + i, 8, stride=64), :] for i in range(8)]
             for i in range(8):
                 p[0, s, x + 1, h * 8 + i + 1] = tiles[i]
-            part[0, s, x, pl.ds(h * 8, 8), :] = sum_rows(tiles)
+            part[0, s, x, pl.ds(h * 8, 8), :] = add_up(
+                [rows_in[s, f, pl.ds(x * 16 + h * 8, 8), :] for f in range(8)]
+            )
 
         return body
 
@@ -439,12 +427,12 @@
         base_weight, section_weight = WEIGHTS[k - 1]
         old = k - 1
         flat = out.reshape(8 * NS * 64, 128)
+        flat_p = p.reshape(3 * NS * 6 * 18 * 8, 128)
 
         def body(x, h):
             y0 = h * 8
             tiles, weights = [[], []], []
             columns = [[p[old, 2 * c + j, x + 1, y0 + i] for i in range(10)] for j in range(2)]
-            means = [mean_row[j, x, pl.ds(y0, 8), :] for j in range(2)]
             for i in range(8):
                 y = y0 + i
                 factor = [coef[d, x, y] for d in range(6)]
@@ -452,7 +440,7 @@
                 here = [columns[j][i + 1] for j in range(2)]
                 new = [
                     keep * here[j]
-                    + spread(means[j], i)
+                    + jnp.broadcast_to(mean_row[j, x, pl.ds(y, 1), :], (8, 128))
                     + factor[0] * p[old, 2 * c + j, x + 2, y + 1]
                     + factor[1] * p[old, 2 * c + j, x, y + 1]
                     + factor[2] * columns[j][i + 2]
@@ -490,7 +478,11 @@
                         flat[pl.ds(s * 64 + x * 16 + y0 + i, 8, stride=NS * 64), :] = tiles[j][i]
             if k < 3:
                 for j in range(2):
-                    part[k, 2 * c + j, x, pl.ds(y0, 8), :] = sum_rows(tiles[j])
+                    s = 2 * c + j
+                    row = (((k * NS + s) * 6 + x + 1) * 18 + y0 + 1) * 8
+                    part[k, s, x, pl.ds(y0, 8), :] = add_up(
+                        [flat_p[pl.ds(row + f, 8, stride=8), :] for f in range(8)]
+                    )
 
         return body
 
@@ -512,11 +504,11 @@
                 scatter(k, c, 3)
                 send_y(k, c)
             if c == 0:
+                pass_on(k - 1, PAIRS - 1)
                 second_exchange(k - 1, PAIRS - 1)
-                pass_on(k - 1, PAIRS - 1)
             elif k < 3:
+                pass_on(k, c - 1)
                 second_exchange(k, c - 1)
-                pass_on(k, c - 1)
             if k < 3:
                 send_x(k, c)
 

time: 41.3 us -> 41.1 us (level)
  no operation moved by 1% of the time
where the time goes in v15:
time: 41.1 us; the launch traced here: 41 us
  Pallas kernels  39.9 us (97%)
  local copies, waits for them, and re-layouts  1.15 us (3%)
    pallas_call x1, Pallas kernels, local(): pl.pallas_call(functools.partial(kernel, counts), out_shape=pltpu.VMEM((8...  39.9 us
    unnamed x1, local copies, waits for them, and re-layouts  1.15 us

profile of v15, /device:TPU:8, one launch (start us, length us, event | category | flops | bytes accessed | tf_op | source)
XLA Modules:
  0.0 41.0 jit_solution(3616114226690662351)
XLA Ops:
  0.0 39.9 %shard_map.46 = f32[8,6,64,128]{3,2,1,0:T(8,128)S(1)} custom-call(f32[8,6,64,128]{3,2,1,0:T(8,128)} %bitcast.4, f32[3,4,16,128]{3,2,1,0:T(8,128)} %velocity_hbm.1, f32[4,16,128]{2,1,0:T(8,128)} %diffusivity_hbm.1, f32[3,8]{1,0:T(4,128)} %bitcast.5), custom_call_target="tpu_custom_call" | custom-call | tf_op jit(solution)/shard_map/pallas_call | solution.py:529
  39.9 1.1 %copy.6 = f32[8,6,4,16,128]{4,3,2,1,0:T(8,128)} copy(f32[8,6,4,16,128]{4,3,2,1,0:T(8,128)S(1)} %bitcast.3) | data formatting | bytes 3145728

commit v16 on v13

--- a/solution.py
+++ b/solution.py
@@ -158,16 +158,17 @@
         else:
             wait_bytes(p.at[:, :, pl.ds(1, 4), 1], send_sem.at[way])
 
-    def x_face(k, c, way, s=None):
+    halves = [(s, y) for s in range(2) for y in (0, 8)]
+
+    def x_face(k, c, way, s, y):
         src, dst = {EAST: (4, 0), WEST: (1, 5)}[way]
-        side = way
-        which = pl.ds(2 * c, 2) if s is None else pl.ds(2 * c + s, 1)
-        to = pl.ds(0, 2) if s is None else pl.ds(s, 1)
+        which, rows = pl.ds(2 * c + s, 1), pl.ds(1 + y, 8)
         if k == 0:
-            refs = fields_hbm.at[:, which, pl.ds(16 * (src - 1), 16)], raw.at[side, c, :, to]
-        else:
-            refs = p.at[k, which, src, pl.ds(1, 16)], p.at[k, which, dst, pl.ds(1, 16)]
-        return refs
+            return (
+                fields_hbm.at[:, which, pl.ds(16 * (src - 1) + y, 8)],
+                raw.at[way, c, :, pl.ds(s, 1), pl.ds(y, 8)],
+            )
+        return p.at[k, which, src, rows], p.at[k, which, dst, rows]
 
     def copy_x(refs, way, recv, to):
         return pltpu.make_async_remote_copy(
@@ -179,8 +180,8 @@
             device_id_type=MESH,
         )
 
-    def relay_at(k, c):
-        return raw_relay.at[c] if k == 0 else relay.at[k - 1, c]
+    def relay_at(k, c, y):
+        return raw_relay.at[c, y // 8] if k == 0 else relay.at[k - 1, c, y // 8]
 
     def send_x(k, c):
         recv = recv_sem.at[k, c, EAST]
@@ -188,7 +189,8 @@
 
             @pl.when(plain[way])
             def _():
-                copy_x(x_face(k, c, way), way, recv, target[way]).start()
+                for s, y in halves:
+                    copy_x(x_face(k, c, way, s, y), way, recv, target[way]).start()
 
         @pl.when(is_mid)
         def _():
@@ -196,11 +198,11 @@
 
                 @pl.when(to_relay[way])
                 def _():
-                    src = x_face(k, c, way, 1)[0]
-                    copy_x(
-                        (src, relay_at(k, c)), way, relay_recv.at[k, c], relay_of[way]
-                    ).start()
-                    copy_x(x_face(k, c, way, 0), way, recv, target[way]).start()
+                    for y in (0, 8):
+                        refs = (x_face(k, c, way, 1, y)[0], relay_at(k, c, y))
+                        copy_x(refs, way, relay_recv.at[k, c], relay_of[way]).start()
+                    for y in (0, 8):
+                        copy_x(x_face(k, c, way, 0, y), way, recv, target[way]).start()
 
     def send_y(k, c):
         for way in (NORTH, SOUTH):
@@ -226,20 +228,20 @@
     def pass_on(k, c):
         @pl.when(is_end)
         def _():
-            here = relay_at(k, c)
-            wait_bytes(here, relay_recv.at[k, c])
+            wait_bytes(raw_relay.at[c] if k == 0 else relay.at[k - 1, c], relay_recv.at[k, c])
             for way in (EAST, WEST):
 
                 @pl.when(is_relay[way])
                 def _():
-                    pltpu.make_async_remote_copy(
-                        src_ref=here,
-                        dst_ref=x_face(k, c, way, 1)[1],
-                        send_sem=relay_send,
-                        recv_sem=recv_sem.at[k, c, EAST],
-                        device_id=relay_to[way],
-                        device_id_type=MESH,
-                    ).start()
+                    for y in (0, 8):
+                        pltpu.make_async_remote_copy(
+                            src_ref=relay_at(k, c, y),
+                            dst_ref=x_face(k, c, way, 1, y)[1],
+                            send_sem=relay_send,
+                            recv_sem=recv_sem.at[k, c, EAST],
+                            device_id=relay_to[way],
+                            device_id_type=MESH,
+                        ).start()
 
     def all_passed_on():
         @pl.when(is_end)
@@ -319,6 +321,8 @@
     send_x(0, 0)
     for way in (EAST, WEST, NORTH, SOUTH):
         pl.when(has[way])(lambda way=way: speed_face(way).start())
+    for c in range(1, PAIRS):
+        send_x(0, c)
 
     def scatter(k, c, owner):
         @pl.when(ax != owner)
@@ -384,10 +388,8 @@
             scatter(0, c, owner)
         send_y(0, c)
         if c > 0:
+            pass_on(0, c - 1)
             second_exchange(0, c - 1)
-            pass_on(0, c - 1)
-        if c + 1 < PAIRS:
-            send_x(0, c + 1)
 
     for copy in own:
         copy.wait()
@@ -508,17 +510,16 @@
                     pl.when(has[back[way]])(lambda way=way: turn_face(c, way))
             planes(0, 3, 2, advance(k, c))
             if k < 3:
+                send_x(k, c)
                 scatter(k, c, 0)
                 scatter(k, c, 3)
                 send_y(k, c)
             if c == 0:
+                pass_on(k - 1, PAIRS - 1)
                 second_exchange(k - 1, PAIRS - 1)
-                pass_on(k - 1, PAIRS - 1)
             elif k < 3:
+                pass_on(k, c - 1)
                 second_exchange(k, c - 1)
-                pass_on(k, c - 1)
-            if k < 3:
-                send_x(k, c)
 
     for way in (EAST, WEST, NORTH, SOUTH):
         pl.when(has[way])(lambda way=way: speed_face(way).wait_send())
@@ -554,9 +555,9 @@
             vmem(4, 16, 128),
             vmem(4, 16, 128),
             vmem(3, 8),
-            vmem(2, PAIRS, 1, 16, 8, 128),
+            vmem(2, PAIRS, 2, 1, 8, 8, 128),
             vmem(2, PAIRS, 8, 2, 16, 128),
-            vmem(PAIRS, 8, 1, 16, 128),
+            vmem(PAIRS, 2, 8, 1, 8, 128),
             dma((NS,)),
             dma((5,)),
             dma,

time: 41.3 us -> 40.1 us (0.971)
  Pallas kernels: 40.1 us -> 38.8 us
    pallas_call x1, Pallas kernels: 40.1 us -> 38.8 us  [local(): pl.pallas_call(functools.partial(kernel, counts), out_shape=pltpu.VMEM((8...]
where the time goes in v16:
time: 40.1 us; the launch traced here: 40 us
  Pallas kernels  38.8 us (97%)
  local copies, waits for them, and re-layouts  1.15 us (3%)
    pallas_call x1, Pallas kernels, local(): pl.pallas_call(functools.partial(kernel, counts), out_shape=pltpu.VMEM((8...  38.8 us
    unnamed x1, local copies, waits for them, and re-layouts  1.15 us

profile of v16, /device:TPU:8, one launch (start us, length us, event | category | flops | bytes accessed | tf_op | source)
XLA Modules:
  0.0 40.0 jit_solution(5709698765598853757)
XLA Ops:
  0.0 38.8 %shard_map.46 = f32[8,6,64,128]{3,2,1,0:T(8,128)S(1)} custom-call(f32[8,6,64,128]{3,2,1,0:T(8,128)} %bitcast.4, f32[3,4,16,128]{3,2,1,0:T(8,128)} %velocity_hbm.1, f32[4,16,128]{2,1,0:T(8,128)} %diffusivity_hbm.1, f32[3,8]{1,0:T(4,128)} %bitcast.5), custom_call_target="tpu_custom_call" | custom-call | tf_op jit(solution)/shard_map/pallas_call | solution.py:538
  38.9 1.1 %copy.6 = f32[8,6,4,16,128]{4,3,2,1,0:T(8,128)} copy(f32[8,6,4,16,128]{4,3,2,1,0:T(8,128)S(1)} %bitcast.3) | data formatting | bytes 3145728

commit v17 on v13

--- a/solution.py
+++ b/solution.py
@@ -223,23 +223,23 @@
         pl.when(both[EAST])(lambda: wait_bytes(two_faces, sem))
         pl.when(jnp.logical_not(both[EAST]))(lambda: wait_bytes(one_face, sem))
 
-    def pass_on(k, c):
-        @pl.when(is_end)
+    def pass_on(n, way):
+        if not 0 <= n < 3 * PAIRS:
+            return
+        k, c = divmod(n, PAIRS)
+
+        @pl.when(is_relay[way])
         def _():
             here = relay_at(k, c)
             wait_bytes(here, relay_recv.at[k, c])
-            for way in (EAST, WEST):
-
-                @pl.when(is_relay[way])
-                def _():
-                    pltpu.make_async_remote_copy(
-                        src_ref=here,
-                        dst_ref=x_face(k, c, way, 1)[1],
-                        send_sem=relay_send,
-                        recv_sem=recv_sem.at[k, c, EAST],
-                        device_id=relay_to[way],
-                        device_id_type=MESH,
-                    ).start()
+            pltpu.make_async_remote_copy(
+                src_ref=here,
+                dst_ref=x_face(k, c, way, 1)[1],
+                send_sem=relay_send,
+                recv_sem=recv_sem.at[k, c, EAST],
+                device_id=relay_to[way],
+                device_id_type=MESH,
+            ).start()
 
     def all_passed_on():
         @pl.when(is_end)
@@ -319,6 +319,8 @@
     send_x(0, 0)
     for way in (EAST, WEST, NORTH, SOUTH):
         pl.when(has[way])(lambda way=way: speed_face(way).start())
+    for c in range(1, PAIRS):
+        send_x(0, c)
 
     def scatter(k, c, owner):
         @pl.when(ax != owner)
@@ -383,11 +385,10 @@
         for owner in range(na):
             scatter(0, c, owner)
         send_y(0, c)
+        pass_on(c - 1, EAST)
+        pass_on(c - 2, WEST)
         if c > 0:
             second_exchange(0, c - 1)
-            pass_on(0, c - 1)
-        if c + 1 < PAIRS:
-            send_x(0, c + 1)
 
     for copy in own:
         copy.wait()
@@ -503,22 +504,21 @@
                 scatter(k, c, 1)
                 scatter(k, c, 2)
             arrived_x(k - 1, c)
+            pass_on(3 * k + c - 1, EAST)
             if k == 1:
                 for way in (EAST, WEST):
                     pl.when(has[back[way]])(lambda way=way: turn_face(c, way))
             planes(0, 3, 2, advance(k, c))
             if k < 3:
+                send_x(k, c)
                 scatter(k, c, 0)
                 scatter(k, c, 3)
                 send_y(k, c)
+            pass_on(3 * k + c - 2, WEST)
             if c == 0:
                 second_exchange(k - 1, PAIRS - 1)
-                pass_on(k - 1, PAIRS - 1)
             elif k < 3:
                 second_exchange(k, c - 1)
-                pass_on(k, c - 1)
-            if k < 3:
-                send_x(k, c)
 
     for way in (EAST, WEST, NORTH, SOUTH):
         pl.when(has[way])(lambda way=way: speed_face(way).wait_send())

time: 41.3 us -> 39.8 us (0.964)
  Pallas kernels: 40.1 us -> 38.2 us
    pallas_call x1, Pallas kernels: 40.1 us -> 38.2 us  [local(): pl.pallas_call(functools.partial(kernel, counts), out_shape=pltpu.VMEM((8...]
where the time goes in v17:
time: 39.8 us; the launch traced here: 39.4 us
  Pallas kernels  38.2 us (96%)
  local copies, waits for them, and re-layouts  1.15 us (3%)
    pallas_call x1, Pallas kernels, local(): pl.pallas_call(functools.partial(kernel, counts), out_shape=pltpu.VMEM((8...  38.2 us
    unnamed x1, local copies, waits for them, and re-layouts  1.15 us

profile of v17, /device:TPU:8, one launch (start us, length us, event | category | flops | bytes accessed | tf_op | source)
XLA Modules:
  0.0 39.4 jit_solution(4714961867767596916)
XLA Ops:
  0.0 38.2 %shard_map.46 = f32[8,6,64,128]{3,2,1,0:T(8,128)S(1)} custom-call(f32[8,6,64,128]{3,2,1,0:T(8,128)} %bitcast.4, f32[3,4,16,128]{3,2,1,0:T(8,128)} %velocity_hbm.1, f32[4,16,128]{2,1,0:T(8,128)} %diffusivity_hbm.1, f32[3,8]{1,0:T(4,128)} %bitcast.5), custom_call_target="tpu_custom_call" | custom-call | tf_op jit(solution)/shard_map/pallas_call | solution.py:537
  38.2 1.1 %copy.6 = f32[8,6,4,16,128]{4,3,2,1,0:T(8,128)} copy(f32[8,6,4,16,128]{4,3,2,1,0:T(8,128)S(1)} %bitcast.3) | data formatting | bytes 3145728

commit v18 on v17

--- a/solution.py
+++ b/solution.py
@@ -13,6 +13,7 @@
 FIELDS = 32
 NS = 6
 PAIRS = 3
+SPLIT = 7
 STEP = 0.3
 MIX = 4.0
 RADIATION = 0.5
@@ -186,9 +187,12 @@
         recv = recv_sem.at[k, c, EAST]
         for way in (EAST, WEST):
 
-            @pl.when(plain[way])
+            @pl.when(plain[way] if 3 * k + c < SPLIT else has[way])
             def _():
                 copy_x(x_face(k, c, way), way, recv, target[way]).start()
+
+        if 3 * k + c >= SPLIT:
+            return
 
         @pl.when(is_mid)
         def _():
@@ -224,7 +228,7 @@
         pl.when(jnp.logical_not(both[EAST]))(lambda: wait_bytes(one_face, sem))
 
     def pass_on(n, way):
-        if not 0 <= n < 3 * PAIRS:
+        if not 0 <= n < SPLIT:
             return
         k, c = divmod(n, PAIRS)
 
@@ -244,7 +248,8 @@
     def all_passed_on():
         @pl.when(is_end)
         def _():
-            wait_bytes(relay, relay_send)
+            wait_bytes(relay.at[0], relay_send)
+            wait_bytes(relay.at[1, pl.ds(0, SPLIT - 2 * PAIRS)], relay_send)
             wait_bytes(raw_relay, relay_send)
 
     def planes(first, step, count, body):
@@ -504,7 +509,6 @@
                 scatter(k, c, 1)
                 scatter(k, c, 2)
             arrived_x(k - 1, c)
-            pass_on(3 * k + c - 1, EAST)
             if k == 1:
                 for way in (EAST, WEST):
                     pl.when(has[back[way]])(lambda way=way: turn_face(c, way))
@@ -514,6 +518,7 @@
                 scatter(k, c, 0)
                 scatter(k, c, 3)
                 send_y(k, c)
+            pass_on(3 * k + c - 1, EAST)
             pass_on(3 * k + c - 2, WEST)
             if c == 0:
                 second_exchange(k - 1, PAIRS - 1)

time: 39.8 us -> 39.8 us (level)
  no operation moved by 1% of the time
where the time goes in v18:
time: 39.8 us; the launch traced here: 39.3 us
  Pallas kernels  38.2 us (96%)
  local copies, waits for them, and re-layouts  1.15 us (3%)
    pallas_call x1, Pallas kernels, local(): pl.pallas_call(functools.partial(kernel, counts), out_shape=pltpu.VMEM((8...  38.2 us
    unnamed x1, local copies, waits for them, and re-layouts  1.15 us

profile of v18, /device:TPU:8, one launch (start us, length us, event | category | flops | bytes accessed | tf_op | source)
XLA Modules:
  0.0 39.3 jit_solution(18020024732009751998)
XLA Ops:
  0.0 38.2 %shard_map.46 = f32[8,6,64,128]{3,2,1,0:T(8,128)S(1)} custom-call(f32[8,6,64,128]{3,2,1,0:T(8,128)} %bitcast.4, f32[3,4,16,128]{3,2,1,0:T(8,128)} %velocity_hbm.1, f32[4,16,128]{2,1,0:T(8,128)} %diffusivity_hbm.1, f32[3,8]{1,0:T(4,128)} %bitcast.5), custom_call_target="tpu_custom_call" | custom-call | tf_op jit(solution)/shard_map/pallas_call | solution.py:542
  38.2 1.1 %copy.6 = f32[8,6,4,16,128]{4,3,2,1,0:T(8,128)} copy(f32[8,6,4,16,128]{4,3,2,1,0:T(8,128)S(1)} %bitcast.3) | data formatting | bytes 3145728

commit v19 on v10

--- a/solution.py
+++ b/solution.py
@@ -201,21 +201,23 @@
             def _():
                 copy_x(x_face(k, c, way), way, recv_sem.at[k, c, way], target[way]).wait_recv()
 
-    def pass_on(k, c):
-        for way in (EAST, WEST):
-
-            @pl.when(is_relay[way])
-            def _():
-                here = relay_at(k, c)
-                pltpu.make_async_copy(here, here, relay_recv.at[k, c]).wait()
-                pltpu.make_async_remote_copy(
-                    src_ref=here,
-                    dst_ref=x_face(k, c, way, 1)[1],
-                    send_sem=relay_send,
-                    recv_sem=recv_sem.at[k, c, way],
-                    device_id=relay_to[way],
-                    device_id_type=MESH,
-                ).start()
+    def pass_on(n, way):
+        if not 0 <= n < 3 * PAIRS:
+            return
+        k, c = divmod(n, PAIRS)
+
+        @pl.when(is_relay[way])
+        def _():
+            here = relay_at(k, c)
+            pltpu.make_async_copy(here, here, relay_recv.at[k, c]).wait()
+            pltpu.make_async_remote_copy(
+                src_ref=here,
+                dst_ref=x_face(k, c, way, 1)[1],
+                send_sem=relay_send,
+                recv_sem=recv_sem.at[k, c, way],
+                device_id=relay_to[way],
+                device_id_type=MESH,
+            ).start()
 
     def all_passed_on():
         for way in (EAST, WEST):
@@ -372,8 +374,9 @@
         send(0, c, SOUTH)
         for owner in range(na):
             scatter(0, c, owner)
+        pass_on(c - 1, EAST)
+        pass_on(c - 2, WEST)
         if c > 0:
-            pass_on(0, c - 1)
             second_exchange(0, c - 1)
 
     for copy in own:
@@ -495,17 +498,17 @@
                 for way in (EAST, WEST):
                     pl.when(has[back[way]])(lambda way=way: turn_face(c, way))
             planes(0, 3, 2, advance(k, c))
+            pass_on(3 * k + c - 1, EAST)
             if k < 3:
                 send_x(k, c)
                 scatter(k, c, 0)
                 scatter(k, c, 3)
                 for way in (NORTH, SOUTH):
                     send(k, c, way)
+            pass_on(3 * k + c - 2, WEST)
             if c == 0:
-                pass_on(k - 1, PAIRS - 1)
                 second_exchange(k - 1, PAIRS - 1)
             elif k < 3:
-                pass_on(k, c - 1)
                 second_exchange(k, c - 1)
 
     for way in (EAST, WEST, NORTH, SOUTH):

time: 39.3 us -> 39.8 us (1.013)
  no operation moved by 1% of the time
where the time goes in v19:
time: 39.8 us; the launch traced here: 39.4 us
  Pallas kernels  38.2 us (96%)
  local copies, waits for them, and re-layouts  1.15 us (3%)
    pallas_call x1, Pallas kernels, local(): pl.pallas_call(functools.partial(kernel, counts), out_shape=pltpu.VMEM((8...  38.2 us
    unnamed x1, local copies, waits for them, and re-layouts  1.15 us

profile of v19, /device:TPU:8, one launch (start us, length us, event | category | flops | bytes accessed | tf_op | source)
XLA Modules:
  0.0 39.4 jit_solution(6637472850811583761)
XLA Ops:
  0.0 38.2 %shard_map.46 = f32[8,6,64,128]{3,2,1,0:T(8,128)S(1)} custom-call(f32[8,6,64,128]{3,2,1,0:T(8,128)} %bitcast.4, f32[3,4,16,128]{3,2,1,0:T(8,128)} %velocity_hbm.1, f32[4,16,128]{2,1,0:T(8,128)} %diffusivity_hbm.1, f32[3,8]{1,0:T(4,128)} %bitcast.5), custom_call_target="tpu_custom_call" | custom-call | tf_op jit(solution)/shard_map/pallas_call | solution.py:528
  38.2 1.1 %copy.6 = f32[8,6,4,16,128]{4,3,2,1,0:T(8,128)} copy(f32[8,6,4,16,128]{4,3,2,1,0:T(8,128)S(1)} %bitcast.3) | data formatting | bytes 3145728

commit v20 on v10

--- a/solution.py
+++ b/solution.py
@@ -351,7 +351,10 @@
             tiles = [flat[pl.ds(start + i, 8, stride=64), :] for i in range(8)]
             for i in range(8):
                 p[0, s, x + 1, h * 8 + i + 1] = tiles[i]
-            part[0, s, x, pl.ds(h * 8, 8), :] = sum_rows(tiles)
+            fields = [rows_in[s, f, pl.ds(x * 16 + h * 8, 8), :] for f in range(8)]
+            while len(fields) > 1:
+                fields = [a + b for a, b in zip(fields[::2], fields[1::2])]
+            part[0, s, x, pl.ds(h * 8, 8), :] = fields[0]
 
         return body
 

time: 39.3 us -> 39.2 us (level)
  no operation moved by 1% of the time
where the time goes in v20:
time: 39.2 us; the launch traced here: 39.1 us
  Pallas kernels  38 us (97%)
  local copies, waits for them, and re-layouts  1.15 us (3%)
    pallas_call x1, Pallas kernels, local(): pl.pallas_call(functools.partial(kernel, counts), out_shape=pltpu.VMEM((8...  38 us
    unnamed x1, local copies, waits for them, and re-layouts  1.15 us

profile of v20, /device:TPU:8, one launch (start us, length us, event | category | flops | bytes accessed | tf_op | source)
XLA Modules:
  0.0 39.1 jit_solution(18089277943137701237)
XLA Ops:
  0.0 38.0 %shard_map.46 = f32[8,6,64,128]{3,2,1,0:T(8,128)S(1)} custom-call(f32[8,6,64,128]{3,2,1,0:T(8,128)} %bitcast.4, f32[3,4,16,128]{3,2,1,0:T(8,128)} %velocity_hbm.1, f32[4,16,128]{2,1,0:T(8,128)} %diffusivity_hbm.1, f32[3,8]{1,0:T(4,128)} %bitcast.5), custom_call_target="tpu_custom_call" | custom-call | tf_op jit(solution)/shard_map/pallas_call | solution.py:528
  38.0 1.1 %copy.6 = f32[8,6,4,16,128]{4,3,2,1,0:T(8,128)} copy(f32[8,6,4,16,128]{4,3,2,1,0:T(8,128)S(1)} %bitcast.3) | data formatting | bytes 3145728
